TPU v7x, 768 devices: a whole 4x8x12 slice. The times are simulated.
768 devices in a mesh: gx: 24 (over z, core), gy: 4 (over x), gz: 8 (over y).
Axes of the slice: x: 4, y: 8, z: 12, core: 2. Of those that a mesh axis runs over, the one named last changes fastest.
Arguments:
- design: float32 [96, 32, 1024], P('gx', 'gy', 'gz'), may hold values from 0.05 to 1
- passive: int32 [96, 32, 1024], P('gx', 'gy', 'gz'), may hold values from 0 to 2, as said below
- fixed: int32 [96, 32, 1024], P('gx', 'gy', 'gz'), may hold values 0 or 1
- state: float32 [3, 96, 32, 1024], P(None, 'gx', 'gy', 'gz'), may hold values from -6 to 6
- adjoint: float32 [3, 96, 32, 1024], P(None, 'gx', 'gy', 'gz'), may hold values from -6 to 6
- resid: float32 [3, 96, 32, 1024], P(None, 'gx', 'gy', 'gz'), may hold values from -10 to 10
Outputs:
- adjoint_new: float32 [3, 96, 32, 1024], P(None, 'gx', 'gy', 'gz')
- resid_new: float32 [3, 96, 32, 1024], P(None, 'gx', 'gy', 'gz')
- design_grad: float32 [96, 32, 1024], P('gx', 'gy', 'gz')
Inputs may be any that keep to these rules, and one draw needn't show every extreme that they name: `passive`: 0 marks a design element, 1 an element held void, 2 one held solid.
All inputs are finite; a program needn't handle non-finite values. No bound on the sum of `fixed` on one device may be relied on, other than what follows from the above.
Results may differ from a plain program's by a relative error of at most 0.0003.
Values sent between devices are 32-bit elements; how exact they have to be, the bound alone decides.
A program may use at most 32 MiB of HBM per device.

v0:
```python
import math

import jax
import jax.numpy as jnp
from jax import lax
from jax.sharding import PartitionSpec as P

stiff_floor = 0.001
damping = 0.6
coarse_damping = 0.5


def extended(cells, sides, width):
    for axis, dim in sides:
        count = lax.axis_size(axis)
        ends = count - 1
        head = lax.slice_in_dim(cells, 0, width, axis=dim)
        tail = lax.slice_in_dim(cells, cells.shape[dim] - width, cells.shape[dim], axis=dim)
        cells = jnp.concatenate(
            [
                lax.ppermute(tail, axis, [(i, (i + 1) % count) for i in range(ends)]),
                cells,
                lax.ppermute(head, axis, [((i + 1) % count, i) for i in range(ends)]),
            ],
            axis=dim,
        )
    return cells


def element_matrix():
    ratio = 0.3
    lame = ratio / ((1.0 + ratio) * (1.0 - 2.0 * ratio))
    shear = 0.5 / (1.0 + ratio)
    elastic = [[0.0] * 6 for number in range(6)]
    for i in range(3):
        for k in range(3):
            elastic[i][k] = lame
    for i in range(3):
        elastic[i][i] = elastic[i][i] + 2.0 * shear
        elastic[3 + i][3 + i] = shear
    signs = [[2 * (a >> 2 & 1) - 1, 2 * (a >> 1 & 1) - 1, 2 * (a & 1) - 1] for a in range(8)]
    point = 1.0 / math.sqrt(3.0)
    matrix = [[0.0] * 24 for number in range(24)]
    for p in (-point, point):
        for q in (-point, point):
            for s in (-point, point):
                local = [p, q, s]
                grads = [[0.0] * 3 for number in range(8)]
                for a in range(8):
                    for k in range(3):
                        value = signs[a][k] / 8.0 * 2.0
                        for m in range(3):
                            if m != k:
                                value = value * (1.0 + signs[a][m] * local[m])
                        grads[a][k] = value
                strain = [[0.0] * 24 for number in range(6)]
                for a in range(8):
                    strain[0][a] = grads[a][0]
                    strain[1][8 + a] = grads[a][1]
                    strain[2][16 + a] = grads[a][2]
                    strain[3][a] = grads[a][1]
                    strain[3][8 + a] = grads[a][0]
                    strain[4][8 + a] = grads[a][2]
                    strain[4][16 + a] = grads[a][1]
                    strain[5][a] = grads[a][2]
                    strain[5][16 + a] = grads[a][0]
                stress = [
                    [sum((elastic[m][n] * strain[n][c] for n in range(6))) for c in range(24)]
                    for m in range(6)
                ]
                for r in range(24):
                    for c in range(24):
                        matrix[r][c] = (
                            matrix[r][c]
                            + sum((strain[m][r] * stress[m][c] for m in range(6))) * 0.125
                        )
    return matrix


def corners():
    return [(a >> 2 & 1, a >> 1 & 1, a & 1) for a in range(8)]


def stencil():
    terms = []
    for i in (-1, 0, 1):
        for j in (-1, 0, 1):
            for k in (-1, 0, 1):
                terms.append((i, j, k, 2.0 - math.sqrt(i * i + j * j + k * k)))
    return terms


def inside_line(place, groups, count, first, length):
    places = place * count + first + jnp.arange(length, dtype=jnp.int32)
    return ((places >= 0) & (places < count * groups)).astype(jnp.float32)


def restrict(field):
    shape = field.shape
    return field.reshape(3, shape[1] // 2, 2, shape[2] // 2, 2, shape[3] // 2, 2).sum(
        axis=(2, 4, 6)
    )


def prolong(field):
    return jnp.repeat(jnp.repeat(jnp.repeat(field, 2, axis=1), 2, axis=2), 2, axis=3)


def flat_stencil(ext):
    extent_x, extent_y, extent_z = (ext.shape[1], ext.shape[2], ext.shape[3])
    plane = extent_y * extent_z
    flat = ext.reshape(ext.shape[0], -1)
    length = flat.shape[1]
    reach = 2 * plane + 2 * extent_z + 2
    usable = length - reach
    total = jnp.zeros((ext.shape[0], usable), jnp.float32)
    for i, j, k, weight in stencil():
        offset = (1 + i) * plane + (1 + j) * extent_z + (1 + k)
        total = total + weight * flat[:, offset : offset + usable]
    total = jnp.pad(total, ((0, 0), (0, reach)))
    whole = total.reshape(ext.shape[0], extent_x, extent_y, extent_z)
    return whole[:, : extent_x - 2, : extent_y - 2, : extent_z - 2]


def corner_offsets(extent_y, extent_z):
    return [i * extent_y * extent_z + j * extent_z + k for i, j, k in corners()]


def flat_energy(first_ext, second_ext, stiffness, low, count_x, count_y, count_z):
    extent_x, extent_y, extent_z = (first_ext.shape[1], first_ext.shape[2], first_ext.shape[3])
    offsets = corner_offsets(extent_y, extent_z)
    first_flat = first_ext.reshape(3, -1)
    second_flat = second_ext.reshape(3, -1)
    length = first_flat.shape[1]
    usable = length - offsets[-1]
    first_el = jnp.stack([first_flat[:, o : o + usable] for o in offsets], 1).reshape(24, usable)
    second_el = jnp.stack([second_flat[:, o : o + usable] for o in offsets], 1).reshape(24, usable)
    product = jnp.dot(stiffness, second_el, precision=lax.Precision.HIGHEST)
    energy = jnp.sum(first_el * product, axis=0)
    energy = jnp.pad(energy, (0, offsets[-1])).reshape(extent_x, extent_y, extent_z)
    return energy[low : low + count_x, low : low + count_y, low : low + count_z]


def body(design, passive, fixed, state, adjoint, resid):
    cells_x, cells_y, cells_z = design.shape
    place_x, place_y, place_z = (lax.axis_index("gx"), lax.axis_index("gy"), lax.axis_index("gz"))
    groups_x, groups_y, groups_z = (lax.axis_size("gx"), lax.axis_size("gy"), lax.axis_size("gz"))
    table = element_matrix()
    stiffness = jnp.asarray(table, dtype=jnp.float32)
    stiff_diag = [[table[8 * c + a][8 * c + a] for a in range(8)] for c in range(3)]
    free = (1 - fixed).astype(jnp.float32)
    masked = jnp.where(passive == 1, 0.0, jnp.where(passive == 2, 1.0, design)).astype(jnp.float32)
    stacked = jnp.concatenate([masked[None], free[None], state], 0)
    beside_all = extended(stacked, (("gx", 1), ("gy", 2), ("gz", 3)), 2)
    state_ext = beside_all[2:5]
    span_x, span_y, span_z = (cells_x + 2, cells_y + 2, cells_z + 2)
    outer = (
        inside_line(place_x, groups_x, cells_x, -2, cells_x + 4)[:, None, None]
        * inside_line(place_y, groups_y, cells_y, -2, cells_y + 4)[None, :, None]
        * inside_line(place_z, groups_z, cells_z, -2, cells_z + 4)[None, None, :]
    )
    smoothed = flat_stencil(jnp.stack([beside_all[0], outer], 0))
    weight_sum = smoothed[1]
    density = smoothed[0] / weight_sum
    elem_in = (
        inside_line(place_x, groups_x, cells_x, -1, span_x)[:, None, None]
        * inside_line(place_y, groups_y, cells_y, -1, span_y)[None, :, None]
        * inside_line(place_z, groups_z, cells_z, -1, span_z)[None, None, :]
    )
    factor = elem_in * (stiff_floor + density**3 * (1.0 - stiff_floor))
    rows = []
    for c in range(3):
        total = jnp.zeros((cells_x, cells_y, cells_z), jnp.float32)
        for a, (i, j, k) in enumerate(corners()):
            total = (
                total
                + float(stiff_diag[c][a])
                * factor[1 - i : 1 - i + cells_x, 1 - j : 1 - j + cells_y, 1 - k : 1 - k + cells_z]
            )
        rows.append(total)
    diagonal = free * jnp.stack(rows, 0) + (1.0 - free)
    keep_x = (jnp.arange(span_x) <= cells_x).astype(jnp.float32)
    keep_y = (jnp.arange(span_y) <= cells_y).astype(jnp.float32)
    keep_z = (jnp.arange(span_z) <= cells_z).astype(jnp.float32)
    factor_flat = (
        factor * keep_x[:, None, None] * keep_y[None, :, None] * keep_z[None, None, :]
    ).reshape(-1)
    offsets = corner_offsets(span_y, span_z)
    length = span_x * span_y * span_z
    usable = length - offsets[-1]
    factor_use = factor_flat[:usable]

    def element_forces(ext_field):
        flat = ext_field.reshape(3, -1)
        gathered = jnp.stack([flat[:, o : o + usable] for o in offsets], 1).reshape(24, usable)
        force = (
            jnp.dot(stiffness, gathered, precision=lax.Precision.HIGHEST).reshape(3, 8, usable)
            * factor_use
        )
        total = jnp.zeros((3, length), jnp.float32)
        for a in range(8):
            total = total + jnp.pad(
                force[:, a], ((0, 0), (offsets[a], length - usable - offsets[a]))
            )
        return total.reshape(3, span_x, span_y, span_z)[
            :, 1 : cells_x + 1, 1 : cells_y + 1, 1 : cells_z + 1
        ]

    def fine_rim(field):
        return extended(field, (("gx", 1), ("gy", 2), ("gz", 3)), 1)

    def operator(field):
        return free * element_forces(fine_rim(free * field)) + (1.0 - free) * field

    first = damping * resid / diagonal
    second_res = resid - operator(first)
    coarse_res = restrict(second_res)
    coarse_diag = restrict(diagonal)
    coarse_first = coarse_damping * coarse_res / coarse_diag
    image_coarse = operator(prolong(coarse_first))
    coarse_fix = coarse_first + coarse_damping * (coarse_res - restrict(image_coarse)) / coarse_diag
    middle = first + prolong(coarse_fix)
    direction = middle + damping * (resid - operator(middle)) / diagonal
    numerator = lax.psum(jnp.sum(resid * direction), ("gx", "gy", "gz"))
    image = operator(direction)
    denominator = lax.psum(jnp.sum(direction * image), ("gx", "gy", "gz"))
    step_size = numerator / denominator
    adjoint_new = adjoint + step_size * direction
    resid_new = resid - step_size * image
    adjoint_ext = extended(adjoint_new, (("gx", 1), ("gy", 2), ("gz", 3)), 2)
    energy = flat_energy(adjoint_ext, state_ext, stiffness, 1, span_x, span_y, span_z)
    sens = elem_in * 3.0 * density**2 * (1.0 - stiff_floor) * energy
    scaled_ext = sens / weight_sum
    grad = flat_stencil(scaled_ext[None])[0]
    design_grad = jnp.where(passive == 0, grad, 0.0).astype(jnp.float32)
    return (adjoint_new, resid_new, design_grad)


def solution(mesh):
    return jax.shard_map(
        body,
        mesh=mesh,
        in_specs=(
            P("gx", "gy", "gz"),
            P("gx", "gy", "gz"),
            P("gx", "gy", "gz"),
            P(None, "gx", "gy", "gz"),
            P(None, "gx", "gy", "gz"),
            P(None, "gx", "gy", "gz"),
        ),
        out_specs=(P(None, "gx", "gy", "gz"), P(None, "gx", "gy", "gz"), P("gx", "gy", "gz")),
        check_vma=False,
    )
```

profile of v0, /device:TPU:1, one launch (start us, length us, event | category | flops | bytes accessed | tf_op | source)
XLA Modules:
  0.0 329.3 jit_solution(3574131075472921362)
XLA Ops:
  2.9 5.4 %collective-permute-start = (f32[5,2,8,128]{3,2,1,0:T(8,128)S(1)}, f32[5,2,8,128]{3,2,1,0:T(8,128)S(1)}, u32[]{:S(2)}, u32[]{:S(2)}) collective-permute-start(f32[5,2,8,128]{3,2,1,0:T(8,128)S(1)} %get-tuple-element.57), channel_id=1, source_target_pairs={{0,32},{32,64},{64,96},{96,128},{128,160},{160,192},{192,224},{224... | collective-permute-start | bytes 122888 | tf_op jit(solution)/shard_map/ppermute | solution.py:21
  8.3 8.3 %collective-permute-start.1 = (f32[5,2,8,128]{3,2,1,0:T(8,128)S(1)}, f32[5,2,8,128]{3,2,1,0:T(8,128)S(1)}, u32[]{:S(2)}, u32[]{:S(2)}) collective-permute-start(f32[5,2,8,128]{3,2,1,0:T(8,128)S(1)} %get-tuple-element.58), channel_id=1, source_target_pairs={{32,0},{64,32},{96,64},{128,96},{160,128},{192,160},{224,192},{256... | collective-permute-start | bytes 122888 | tf_op jit(solution)/shard_map/ppermute | solution.py:23
  21.2 3.4 %collective-permute-done.3 = f32[5,8,2,128]{3,2,1,0:T(2,128)S(1)} collective-permute-done((f32[5,8,2,128]{3,2,1,0:T(2,128)S(1)}, f32[5,8,2,128]{3,2,1,0:T(2,128)S(1)}, u32[]{:S(2)}, u32[]{:S(2)}) %collective-permute-start.3) | collective-permute-done | bytes 40992 | tf_op jit(solution)/shard_map/ppermute | solution.py:23
  29.2 3.5 %collective-permute-done.4 = f32[5,8,12,2]{3,2,1,0:T(8,128)S(1)} collective-permute-done((f32[5,8,12,2]{3,2,1,0:T(8,128)S(1)}, f32[5,8,12,2]{3,2,1,0:T(8,128)S(1)}, u32[]{:S(2)}, u32[]{:S(2)}) %collective-permute-start.4) | collective-permute-done | bytes 3872 | tf_op jit(solution)/shard_map/ppermute | solution.py:21
  32.7 3.9 %collective-permute-done.5 = f32[5,8,12,2]{3,2,1,0:T(8,128)S(1)} collective-permute-done((f32[5,8,12,2]{3,2,1,0:T(8,128)S(1)}, f32[5,8,12,2]{3,2,1,0:T(8,128)S(1)}, u32[]{:S(2)}, u32[]{:S(2)}) %collective-permute-start.5) | collective-permute-done | bytes 3872 | tf_op jit(solution)/shard_map/ppermute | solution.py:23
  38.1 4.1 %fusion.68 = f32[2,9238]{1,0:T(2,128)S(1)} fusion(f32[1,12672]{1,0:T(1,128)S(1)} %stack.172, f32[1,12672]{1,0:T(1,128)S(1)} %mul.478), kind=kLoop, calls=%fused_computation.230 | loop fusion | flops 1367224 | bytes 175280 | tf_op jit(solution)/shard_map/add | solution.py:119
  42.7 6.2 %collective-permute-start.6 = (f32[3,1,8,128]{3,2,1,0:T(8,128)S(1)}, f32[3,1,8,128]{3,2,1,0:T(8,128)S(1)}, u32[]{:S(2)}, u32[]{:S(2)}) collective-permute-start(f32[3,1,8,128]{3,2,1,0:T(8,128)S(1)} %get-tuple-element.77), channel_id=1, source_target_pairs={{0,32},{32,64},{64,96},{96,128},{128,160},{160,192},{192,224},{224... | collective-permute-start | bytes 36872 | tf_op jit(solution)/shard_map/ppermute | solution.py:21
  51.0 2.8 collective-permute-done.7
  53.9 3.1 collective-permute-start.8
  58.5 2.9 collective-permute-done.9
  61.6 3.2 collective-permute-start.10
  68.4 4.7 %collective-permute-done.11 = f32[3,6,10,1]{3,2,1,0:T(8,128)S(1)} collective-permute-done((f32[3,6,10,1]{3,2,1,0:T(8,128)S(1)}, f32[3,6,10,1]{3,2,1,0:T(8,128)S(1)}, u32[]{:S(2)}, u32[]{:S(2)}) %collective-permute-start.11) | collective-permute-done | bytes 752 | tf_op jit(solution)/shard_map/ppermute | solution.py:23
  77.3 3.9 %reshape.277 = f32[3,2,2,4,2,64,2]{6,5,4,3,2,1,0:T(8,128)S(1)} reshape(f32[3,4,8,128]{3,2,1,0:T(8,128)} %fusion.146) | data formatting | bytes 98304 | tf_op jit(solution)/shard_map/reshape | solution.py:100
  83.5 4.3 %collective-permute-start.12 = (f32[3,1,8,128]{3,2,1,0:T(8,128)S(1)}, f32[3,1,8,128]{3,2,1,0:T(8,128)S(1)}, u32[]{:S(2)}, u32[]{:S(2)}) collective-permute-start(f32[3,1,8,128]{3,2,1,0:T(8,128)S(1)} %get-tuple-element.75), channel_id=1, source_target_pairs={{0,32},{32,64},{64,96},{96,128},{128,160},{160,192},{192,224},{224... | collective-permute-start | bytes 36872 | tf_op jit(solution)/shard_map/ppermute | solution.py:21
  89.8 3.1 collective-permute-done.13
  97.0 3.1 collective-permute-done.15
  100.2 4.8 %collective-permute-start.16 = (f32[3,6,10,1]{3,2,1,0:T(8,128)S(1)}, f32[3,6,10,1]{3,2,1,0:T(8,128)S(1)}, u32[]{:S(2)}, u32[]{:S(2)}) collective-permute-start(f32[3,6,10,1]{3,2,1,0:T(8,128)S(1)} %get-tuple-element.51), channel_id=1, source_target_pairs={{0,1},{1,2},{2,3},{3,4},{4,5},{5,6},{6,7},{8,9},{9,10},{10,11},{11... | collective-permute-start | bytes 2168 | tf_op jit(solution)/shard_map/ppermute | solution.py:21
  108.6 4.0 %collective-permute-done.17 = f32[3,6,10,1]{3,2,1,0:T(8,128)S(1)} collective-permute-done((f32[3,6,10,1]{3,2,1,0:T(8,128)S(1)}, f32[3,6,10,1]{3,2,1,0:T(8,128)S(1)}, u32[]{:S(2)}, u32[]{:S(2)}) %collective-permute-start.17) | collective-permute-done | bytes 752 | tf_op jit(solution)/shard_map/ppermute | solution.py:23
  116.8 3.9 %reshape.285 = f32[3,2,2,4,2,64,2]{6,5,4,3,2,1,0:T(8,128)S(1)} reshape(f32[3,4,8,128]{3,2,1,0:T(8,128)} %fusion.144) | data formatting | bytes 98304 | tf_op jit(solution)/shard_map/reshape | solution.py:100
  123.1 4.4 %collective-permute-start.18 = (f32[3,1,8,128]{3,2,1,0:T(8,128)S(1)}, f32[3,1,8,128]{3,2,1,0:T(8,128)S(1)}, u32[]{:S(2)}, u32[]{:S(2)}) collective-permute-start(f32[3,1,8,128]{3,2,1,0:T(8,128)S(1)} %get-tuple-element.73), channel_id=1, source_target_pairs={{0,32},{32,64},{64,96},{96,128},{128,160},{160,192},{192,224},{224... | collective-permute-start | bytes 36872 | tf_op jit(solution)/shard_map/ppermute | solution.py:21
  129.4 3.1 collective-permute-done.19
  138.9 3.4 %collective-permute-start.22 = (f32[3,6,10,1]{3,2,1,0:T(8,128)S(1)}, f32[3,6,10,1]{3,2,1,0:T(8,128)S(1)}, u32[]{:S(2)}, u32[]{:S(2)}) collective-permute-start(f32[3,6,10,1]{3,2,1,0:T(8,128)S(1)} %get-tuple-element.49), channel_id=1, source_target_pairs={{0,1},{1,2},{2,3},{3,4},{4,5},{5,6},{6,7},{8,9},{9,10},{10,11},{11... | collective-permute-start | bytes 2168 | tf_op jit(solution)/shard_map/ppermute | solution.py:21
  146.0 3.9 %collective-permute-done.23 = f32[3,6,10,1]{3,2,1,0:T(8,128)S(1)} collective-permute-done((f32[3,6,10,1]{3,2,1,0:T(8,128)S(1)}, f32[3,6,10,1]{3,2,1,0:T(8,128)S(1)}, u32[]{:S(2)}, u32[]{:S(2)}) %collective-permute-start.23) | collective-permute-done | bytes 752 | tf_op jit(solution)/shard_map/ppermute | solution.py:23
  153.5 5.7 %collective-permute-start.24 = (f32[3,1,8,128]{3,2,1,0:T(8,128)S(1)}, f32[3,1,8,128]{3,2,1,0:T(8,128)S(1)}, u32[]{:S(2)}, u32[]{:S(2)}) collective-permute-start(f32[3,1,8,128]{3,2,1,0:T(8,128)S(1)} %get-tuple-element.71), channel_id=1, source_target_pairs={{0,32},{32,64},{64,96},{96,128},{128,160},{160,192},{192,224},{224... | collective-permute-start | bytes 36872 | tf_op jit(solution)/shard_map/ppermute | solution.py:21
  161.3 2.9 collective-permute-done.25
  167.5 2.9 collective-permute-done.27
  176.7 3.9 %collective-permute-done.29 = f32[3,6,10,1]{3,2,1,0:T(8,128)S(1)} collective-permute-done((f32[3,6,10,1]{3,2,1,0:T(8,128)S(1)}, f32[3,6,10,1]{3,2,1,0:T(8,128)S(1)}, u32[]{:S(2)}, u32[]{:S(2)}) %collective-permute-start.29) | collective-permute-done | bytes 752 | tf_op jit(solution)/shard_map/ppermute | solution.py:23
  184.8 111.0 %all-reduce.35 = (f32[]{:T(128)}, f32[]{:T(128)}) all-reduce(f32[]{:T(128)} %get-tuple-element.4, f32[]{:T(128)} %get-tuple-element.3), channel_id=1, replica_groups=mesh['gx'=24,'gy'=4,'gz'=8] {'gx','gy','gz'}, use_global_device_ids=true, to_apply=%region_4.5 | all-reduce | flops 2 | bytes 16 | tf_op jit(solution)/shard_map/psum | solution.py:224
  305.0 3.7 %collective-permute-start.32 = (f32[3,8,2,128]{3,2,1,0:T(2,128)S(1)}, f32[3,8,2,128]{3,2,1,0:T(2,128)S(1)}, u32[]{:S(2)}, u32[]{:S(2)}) collective-permute-start(f32[3,8,2,128]{3,2,1,0:T(2,128)S(1)} %get-tuple-element.55), channel_id=1, source_target_pairs={{0,8},{8,16},{16,24},{1,9},{9,17},{17,25},{2,10},{10,18},{18,26},{... | collective-permute-start | bytes 73736 | tf_op jit(solution)/shard_map/ppermute | solution.py:21
  310.2 3.1 collective-permute-done.33
  316.2 3.2 collective-permute-done.34
  319.4 3.9 %collective-permute-done.35 = f32[3,8,12,2]{3,2,1,0:T(8,128)S(1)} collective-permute-done((f32[3,8,12,2]{3,2,1,0:T(8,128)S(1)}, f32[3,8,12,2]{3,2,1,0:T(8,128)S(1)}, u32[]{:S(2)}, u32[]{:S(2)}) %collective-permute-start.35) | collective-permute-done | bytes 2336 | tf_op jit(solution)/shard_map/ppermute | solution.py:23
  (239 shorter events, 92.3 us)
Async XLA Ops:
  2.9 14.1 %collective-permute-start = (f32[5,2,8,128]{3,2,1,0:T(8,128)S(1)}, f32[5,2,8,128]{3,2,1,0:T(8,128)S(1)}, u32[]{:S(2)}, u32[]{:S(2)}) collective-permute-start(f32[5,2,8,128]{3,2,1,0:T(8,128)S(1)} %get-tuple-element.57), channel_id=1, source_target_pairs={{0,32},{32,64},{64,96},{96,128},{128,160},{160,192},{192,224},{224... | collective-permute-start | bytes 122888 | tf_op jit(solution)/shard_map/ppermute | solution.py:21
  8.3 9.2 %collective-permute-start.1 = (f32[5,2,8,128]{3,2,1,0:T(8,128)S(1)}, f32[5,2,8,128]{3,2,1,0:T(8,128)S(1)}, u32[]{:S(2)}, u32[]{:S(2)}) collective-permute-start(f32[5,2,8,128]{3,2,1,0:T(8,128)S(1)} %get-tuple-element.58), channel_id=1, source_target_pairs={{32,0},{64,32},{96,64},{128,96},{160,128},{192,160},{224,192},{256... | collective-permute-start | bytes 122888 | tf_op jit(solution)/shard_map/ppermute | solution.py:23
  19.8 4.7 %collective-permute-start.3 = (f32[5,8,2,128]{3,2,1,0:T(2,128)S(1)}, f32[5,8,2,128]{3,2,1,0:T(2,128)S(1)}, u32[]{:S(2)}, u32[]{:S(2)}) collective-permute-start(f32[5,8,2,128]{3,2,1,0:T(2,128)S(1)} %get-tuple-element.46), channel_id=1, source_target_pairs={{8,0},{16,8},{24,16},{9,1},{17,9},{25,17},{10,2},{18,10},{26,18},{... | collective-permute-start | bytes 122888 | tf_op jit(solution)/shard_map/ppermute | solution.py:23
  25.6 7.1 %collective-permute-start.4 = (f32[5,8,12,2]{3,2,1,0:T(8,128)S(1)}, f32[5,8,12,2]{3,2,1,0:T(8,128)S(1)}, u32[]{:S(2)}, u32[]{:S(2)}) collective-permute-start(f32[5,8,12,2]{3,2,1,0:T(8,128)S(1)} %get-tuple-element.41), channel_id=1, source_target_pairs={{0,1},{1,2},{2,3},{3,4},{4,5},{5,6},{6,7},{8,9},{9,10},{10,11},{11... | collective-permute-start | bytes 11528 | tf_op jit(solution)/shard_map/ppermute | solution.py:21
  26.9 9.6 %collective-permute-start.5 = (f32[5,8,12,2]{3,2,1,0:T(8,128)S(1)}, f32[5,8,12,2]{3,2,1,0:T(8,128)S(1)}, u32[]{:S(2)}, u32[]{:S(2)}) collective-permute-start(f32[5,8,12,2]{3,2,1,0:T(8,128)S(1)} %get-tuple-element.42), channel_id=1, source_target_pairs={{1,0},{2,1},{3,2},{4,3},{5,4},{6,5},{7,6},{9,8},{10,9},{11,10},{12... | collective-permute-start | bytes 11528 | tf_op jit(solution)/shard_map/ppermute | solution.py:23
  42.7 8.3 %collective-permute-start.6 = (f32[3,1,8,128]{3,2,1,0:T(8,128)S(1)}, f32[3,1,8,128]{3,2,1,0:T(8,128)S(1)}, u32[]{:S(2)}, u32[]{:S(2)}) collective-permute-start(f32[3,1,8,128]{3,2,1,0:T(8,128)S(1)} %get-tuple-element.77), channel_id=1, source_target_pairs={{0,32},{32,64},{64,96},{96,128},{128,160},{160,192},{192,224},{224... | collective-permute-start | bytes 36872 | tf_op jit(solution)/shard_map/ppermute | solution.py:21
  48.9 5.0 %collective-permute-start.7 = (f32[3,1,8,128]{3,2,1,0:T(8,128)S(1)}, f32[3,1,8,128]{3,2,1,0:T(8,128)S(1)}, u32[]{:S(2)}, u32[]{:S(2)}) collective-permute-start(f32[3,1,8,128]{3,2,1,0:T(8,128)S(1)} %get-tuple-element.78), channel_id=1, source_target_pairs={{32,0},{64,32},{96,64},{128,96},{160,128},{192,160},{224,192},{256... | collective-permute-start | bytes 36872 | tf_op jit(solution)/shard_map/ppermute | solution.py:23
  53.9 4.6 %collective-permute-start.8 = (f32[3,6,1,128]{3,2,1,0:T(1,128)S(1)}, f32[3,6,1,128]{3,2,1,0:T(1,128)S(1)}, u32[]{:S(2)}, u32[]{:S(2)}) collective-permute-start(f32[3,6,1,128]{3,2,1,0:T(1,128)S(1)} %get-tuple-element.65), channel_id=1, source_target_pairs={{0,8},{8,16},{16,24},{1,9},{9,17},{17,25},{2,10},{10,18},{18,26},{... | collective-permute-start | bytes 27656 | tf_op jit(solution)/shard_map/ppermute | solution.py:21
  57.0 4.4 %collective-permute-start.9 = (f32[3,6,1,128]{3,2,1,0:T(1,128)S(1)}, f32[3,6,1,128]{3,2,1,0:T(1,128)S(1)}, u32[]{:S(2)}, u32[]{:S(2)}) collective-permute-start(f32[3,6,1,128]{3,2,1,0:T(1,128)S(1)} %get-tuple-element.66), channel_id=1, source_target_pairs={{8,0},{16,8},{24,16},{9,1},{17,9},{25,17},{10,2},{18,10},{26,18},{... | collective-permute-start | bytes 27656 | tf_op jit(solution)/shard_map/ppermute | solution.py:23
  61.6 6.8 %collective-permute-start.10 = (f32[3,6,10,1]{3,2,1,0:T(8,128)S(1)}, f32[3,6,10,1]{3,2,1,0:T(8,128)S(1)}, u32[]{:S(2)}, u32[]{:S(2)}) collective-permute-start(f32[3,6,10,1]{3,2,1,0:T(8,128)S(1)} %get-tuple-element.53), channel_id=1, source_target_pairs={{0,1},{1,2},{2,3},{3,4},{4,5},{5,6},{6,7},{8,9},{9,10},{10,11},{11... | collective-permute-start | bytes 2168 | tf_op jit(solution)/shard_map/ppermute | solution.py:21
  64.8 8.4 %collective-permute-start.11 = (f32[3,6,10,1]{3,2,1,0:T(8,128)S(1)}, f32[3,6,10,1]{3,2,1,0:T(8,128)S(1)}, u32[]{:S(2)}, u32[]{:S(2)}) collective-permute-start(f32[3,6,10,1]{3,2,1,0:T(8,128)S(1)} %get-tuple-element.54), channel_id=1, source_target_pairs={{1,0},{2,1},{3,2},{4,3},{5,4},{6,5},{7,6},{9,8},{10,9},{11,10},{12... | collective-permute-start | bytes 2168 | tf_op jit(solution)/shard_map/ppermute | solution.py:23
  83.5 6.2 %collective-permute-start.12 = (f32[3,1,8,128]{3,2,1,0:T(8,128)S(1)}, f32[3,1,8,128]{3,2,1,0:T(8,128)S(1)}, u32[]{:S(2)}, u32[]{:S(2)}) collective-permute-start(f32[3,1,8,128]{3,2,1,0:T(8,128)S(1)} %get-tuple-element.75), channel_id=1, source_target_pairs={{0,32},{32,64},{64,96},{96,128},{128,160},{160,192},{192,224},{224... | collective-permute-start | bytes 36872 | tf_op jit(solution)/shard_map/ppermute | solution.py:21
  87.8 5.0 %collective-permute-start.13 = (f32[3,1,8,128]{3,2,1,0:T(8,128)S(1)}, f32[3,1,8,128]{3,2,1,0:T(8,128)S(1)}, u32[]{:S(2)}, u32[]{:S(2)}) collective-permute-start(f32[3,1,8,128]{3,2,1,0:T(8,128)S(1)} %get-tuple-element.76), channel_id=1, source_target_pairs={{32,0},{64,32},{96,64},{128,96},{160,128},{192,160},{224,192},{256... | collective-permute-start | bytes 36872 | tf_op jit(solution)/shard_map/ppermute | solution.py:23
  95.7 4.4 %collective-permute-start.15 = (f32[3,6,1,128]{3,2,1,0:T(1,128)S(1)}, f32[3,6,1,128]{3,2,1,0:T(1,128)S(1)}, u32[]{:S(2)}, u32[]{:S(2)}) collective-permute-start(f32[3,6,1,128]{3,2,1,0:T(1,128)S(1)} %get-tuple-element.64), channel_id=1, source_target_pairs={{8,0},{16,8},{24,16},{9,1},{17,9},{25,17},{10,2},{18,10},{26,18},{... | collective-permute-start | bytes 27656 | tf_op jit(solution)/shard_map/ppermute | solution.py:23
  100.2 8.4 %collective-permute-start.16 = (f32[3,6,10,1]{3,2,1,0:T(8,128)S(1)}, f32[3,6,10,1]{3,2,1,0:T(8,128)S(1)}, u32[]{:S(2)}, u32[]{:S(2)}) collective-permute-start(f32[3,6,10,1]{3,2,1,0:T(8,128)S(1)} %get-tuple-element.51), channel_id=1, source_target_pairs={{0,1},{1,2},{2,3},{3,4},{4,5},{5,6},{6,7},{8,9},{9,10},{10,11},{11... | collective-permute-start | bytes 2168 | tf_op jit(solution)/shard_map/ppermute | solution.py:21
  105.0 7.7 %collective-permute-start.17 = (f32[3,6,10,1]{3,2,1,0:T(8,128)S(1)}, f32[3,6,10,1]{3,2,1,0:T(8,128)S(1)}, u32[]{:S(2)}, u32[]{:S(2)}) collective-permute-start(f32[3,6,10,1]{3,2,1,0:T(8,128)S(1)} %get-tuple-element.52), channel_id=1, source_target_pairs={{1,0},{2,1},{3,2},{4,3},{5,4},{6,5},{7,6},{9,8},{10,9},{11,10},{12... | collective-permute-start | bytes 2168 | tf_op jit(solution)/shard_map/ppermute | solution.py:23
  123.1 6.3 %collective-permute-start.18 = (f32[3,1,8,128]{3,2,1,0:T(8,128)S(1)}, f32[3,1,8,128]{3,2,1,0:T(8,128)S(1)}, u32[]{:S(2)}, u32[]{:S(2)}) collective-permute-start(f32[3,1,8,128]{3,2,1,0:T(8,128)S(1)} %get-tuple-element.73), channel_id=1, source_target_pairs={{0,32},{32,64},{64,96},{96,128},{128,160},{160,192},{192,224},{224... | collective-permute-start | bytes 36872 | tf_op jit(solution)/shard_map/ppermute | solution.py:21
  127.5 5.0 %collective-permute-start.19 = (f32[3,1,8,128]{3,2,1,0:T(8,128)S(1)}, f32[3,1,8,128]{3,2,1,0:T(8,128)S(1)}, u32[]{:S(2)}, u32[]{:S(2)}) collective-permute-start(f32[3,1,8,128]{3,2,1,0:T(8,128)S(1)} %get-tuple-element.74), channel_id=1, source_target_pairs={{32,0},{64,32},{96,64},{128,96},{160,128},{192,160},{224,192},{256... | collective-permute-start | bytes 36872 | tf_op jit(solution)/shard_map/ppermute | solution.py:23
  134.4 4.4 %collective-permute-start.21 = (f32[3,6,1,128]{3,2,1,0:T(1,128)S(1)}, f32[3,6,1,128]{3,2,1,0:T(1,128)S(1)}, u32[]{:S(2)}, u32[]{:S(2)}) collective-permute-start(f32[3,6,1,128]{3,2,1,0:T(1,128)S(1)} %get-tuple-element.62), channel_id=1, source_target_pairs={{8,0},{16,8},{24,16},{9,1},{17,9},{25,17},{10,2},{18,10},{26,18},{... | collective-permute-start | bytes 27656 | tf_op jit(solution)/shard_map/ppermute | solution.py:23
  138.9 7.1 %collective-permute-start.22 = (f32[3,6,10,1]{3,2,1,0:T(8,128)S(1)}, f32[3,6,10,1]{3,2,1,0:T(8,128)S(1)}, u32[]{:S(2)}, u32[]{:S(2)}) collective-permute-start(f32[3,6,10,1]{3,2,1,0:T(8,128)S(1)} %get-tuple-element.49), channel_id=1, source_target_pairs={{0,1},{1,2},{2,3},{3,4},{4,5},{5,6},{6,7},{8,9},{9,10},{10,11},{11... | collective-permute-start | bytes 2168 | tf_op jit(solution)/shard_map/ppermute | solution.py:21
  142.4 7.5 %collective-permute-start.23 = (f32[3,6,10,1]{3,2,1,0:T(8,128)S(1)}, f32[3,6,10,1]{3,2,1,0:T(8,128)S(1)}, u32[]{:S(2)}, u32[]{:S(2)}) collective-permute-start(f32[3,6,10,1]{3,2,1,0:T(8,128)S(1)} %get-tuple-element.50), channel_id=1, source_target_pairs={{1,0},{2,1},{3,2},{4,3},{5,4},{6,5},{7,6},{9,8},{10,9},{11,10},{12... | collective-permute-start | bytes 2168 | tf_op jit(solution)/shard_map/ppermute | solution.py:23
  153.5 7.8 %collective-permute-start.24 = (f32[3,1,8,128]{3,2,1,0:T(8,128)S(1)}, f32[3,1,8,128]{3,2,1,0:T(8,128)S(1)}, u32[]{:S(2)}, u32[]{:S(2)}) collective-permute-start(f32[3,1,8,128]{3,2,1,0:T(8,128)S(1)} %get-tuple-element.71), channel_id=1, source_target_pairs={{0,32},{32,64},{64,96},{96,128},{128,160},{160,192},{192,224},{224... | collective-permute-start | bytes 36872 | tf_op jit(solution)/shard_map/ppermute | solution.py:21
  159.1 5.0 %collective-permute-start.25 = (f32[3,1,8,128]{3,2,1,0:T(8,128)S(1)}, f32[3,1,8,128]{3,2,1,0:T(8,128)S(1)}, u32[]{:S(2)}, u32[]{:S(2)}) collective-permute-start(f32[3,1,8,128]{3,2,1,0:T(8,128)S(1)} %get-tuple-element.72), channel_id=1, source_target_pairs={{32,0},{64,32},{96,64},{128,96},{160,128},{192,160},{224,192},{256... | collective-permute-start | bytes 36872 | tf_op jit(solution)/shard_map/ppermute | solution.py:23
  166.0 4.4 %collective-permute-start.27 = (f32[3,6,1,128]{3,2,1,0:T(1,128)S(1)}, f32[3,6,1,128]{3,2,1,0:T(1,128)S(1)}, u32[]{:S(2)}, u32[]{:S(2)}) collective-permute-start(f32[3,6,1,128]{3,2,1,0:T(1,128)S(1)} %get-tuple-element.60), channel_id=1, source_target_pairs={{8,0},{16,8},{24,16},{9,1},{17,9},{25,17},{10,2},{18,10},{26,18},{... | collective-permute-start | bytes 27656 | tf_op jit(solution)/shard_map/ppermute | solution.py:23
  170.6 6.2 %collective-permute-start.28 = (f32[3,6,10,1]{3,2,1,0:T(8,128)S(1)}, f32[3,6,10,1]{3,2,1,0:T(8,128)S(1)}, u32[]{:S(2)}, u32[]{:S(2)}) collective-permute-start(f32[3,6,10,1]{3,2,1,0:T(8,128)S(1)} %get-tuple-element.47), channel_id=1, source_target_pairs={{0,1},{1,2},{2,3},{3,4},{4,5},{5,6},{6,7},{8,9},{9,10},{10,11},{11... | collective-permute-start | bytes 2168 | tf_op jit(solution)/shard_map/ppermute | solution.py:21
  173.1 7.5 %collective-permute-start.29 = (f32[3,6,10,1]{3,2,1,0:T(8,128)S(1)}, f32[3,6,10,1]{3,2,1,0:T(8,128)S(1)}, u32[]{:S(2)}, u32[]{:S(2)}) collective-permute-start(f32[3,6,10,1]{3,2,1,0:T(8,128)S(1)} %get-tuple-element.48), channel_id=1, source_target_pairs={{1,0},{2,1},{3,2},{4,3},{5,4},{6,5},{7,6},{9,8},{10,9},{11,10},{12... | collective-permute-start | bytes 2168 | tf_op jit(solution)/shard_map/ppermute | solution.py:23
  297.9 4.5 %collective-permute-start.30 = (f32[3,2,8,128]{3,2,1,0:T(8,128)S(1)}, f32[3,2,8,128]{3,2,1,0:T(8,128)S(1)}, u32[]{:S(2)}, u32[]{:S(2)}) collective-permute-start(f32[3,2,8,128]{3,2,1,0:T(8,128)S(1)} %get-tuple-element.67), channel_id=1, source_target_pairs={{0,32},{32,64},{64,96},{96,128},{128,160},{160,192},{192,224},{224... | collective-permute-start | bytes 73736 | tf_op jit(solution)/shard_map/ppermute | solution.py:21
  299.9 5.1 %collective-permute-start.31 = (f32[3,2,8,128]{3,2,1,0:T(8,128)S(1)}, f32[3,2,8,128]{3,2,1,0:T(8,128)S(1)}, u32[]{:S(2)}, u32[]{:S(2)}) collective-permute-start(f32[3,2,8,128]{3,2,1,0:T(8,128)S(1)} %get-tuple-element.68), channel_id=1, source_target_pairs={{32,0},{64,32},{96,64},{128,96},{160,128},{192,160},{224,192},{256... | collective-permute-start | bytes 73736 | tf_op jit(solution)/shard_map/ppermute | solution.py:23
  305.0 5.2 %collective-permute-start.32 = (f32[3,8,2,128]{3,2,1,0:T(2,128)S(1)}, f32[3,8,2,128]{3,2,1,0:T(2,128)S(1)}, u32[]{:S(2)}, u32[]{:S(2)}) collective-permute-start(f32[3,8,2,128]{3,2,1,0:T(2,128)S(1)} %get-tuple-element.55), channel_id=1, source_target_pairs={{0,8},{8,16},{16,24},{1,9},{9,17},{17,25},{2,10},{10,18},{18,26},{... | collective-permute-start | bytes 73736 | tf_op jit(solution)/shard_map/ppermute | solution.py:21
  308.7 4.6 %collective-permute-start.33 = (f32[3,8,2,128]{3,2,1,0:T(2,128)S(1)}, f32[3,8,2,128]{3,2,1,0:T(2,128)S(1)}, u32[]{:S(2)}, u32[]{:S(2)}) collective-permute-start(f32[3,8,2,128]{3,2,1,0:T(2,128)S(1)} %get-tuple-element.56), channel_id=1, source_target_pairs={{8,0},{16,8},{24,16},{9,1},{17,9},{25,17},{10,2},{18,10},{26,18},{... | collective-permute-start | bytes 73736 | tf_op jit(solution)/shard_map/ppermute | solution.py:23
  313.4 6.0 %collective-permute-start.34 = (f32[3,8,12,2]{3,2,1,0:T(8,128)S(1)}, f32[3,8,12,2]{3,2,1,0:T(8,128)S(1)}, u32[]{:S(2)}, u32[]{:S(2)}) collective-permute-start(f32[3,8,12,2]{3,2,1,0:T(8,128)S(1)} %get-tuple-element.43), channel_id=1, source_target_pairs={{0,1},{1,2},{2,3},{3,4},{4,5},{5,6},{6,7},{8,9},{9,10},{10,11},{11... | collective-permute-start | bytes 6920 | tf_op jit(solution)/shard_map/ppermute | solution.py:21
  314.7 8.6 %collective-permute-start.35 = (f32[3,8,12,2]{3,2,1,0:T(8,128)S(1)}, f32[3,8,12,2]{3,2,1,0:T(8,128)S(1)}, u32[]{:S(2)}, u32[]{:S(2)}) collective-permute-start(f32[3,8,12,2]{3,2,1,0:T(8,128)S(1)} %get-tuple-element.44), channel_id=1, source_target_pairs={{1,0},{2,1},{3,2},{4,3},{5,4},{6,5},{7,6},{9,8},{10,9},{11,10},{12... | collective-permute-start | bytes 6920 | tf_op jit(solution)/shard_map/ppermute | solution.py:23
  (17 other events, 270.1 us)
where the time goes:
time: 334 us; the launch traced here: 329 us
  blocking collectives  111 us (33%)
  starting transfers between devices  93.6 us (28%)
  waiting for transfers between devices  71.3 us (21%)
  local copies, waits for them, and re-layouts  23.9 us (7%)
  other arithmetic  22 us (7%)
  matrix products  3.88 us (1%)
  between operations  3.55 us (1%)
    psum x1, blocking collectives, body(): numerator = lax.psum(jnp.sum(resid * direction), ('gx', 'gy', 'gz'))  111 us
    ppermute x18, starting transfers between devices, extended(): lax.ppermute(tail, axis, [(i, (i + 1) % count) for i in range(ends)])  59.1 us
    ppermute x18, waiting for transfers between devices, extended(): lax.ppermute(head, axis, [((i + 1) % count, i) for i in range(ends)])  57.4 us
    ppermute x18, starting transfers between devices, extended(): lax.ppermute(head, axis, [((i + 1) % count, i) for i in range(ends)])  34.5 us
    ppermute x18, waiting for transfers between devices, extended(): lax.ppermute(tail, axis, [(i, (i + 1) % count) for i in range(ends)])  13.9 us
    reshape x2, local copies, waits for them, and re-layouts, restrict(): field.reshape(3, shape[1] // 2, 2, shape[2] // 2, 2, shape[3] // 2, 2)  7.77 us
  transfers between devices with their start and end apart: 36, of which 24 were waited for; matrix products, arithmetic and copies ran while one was open for 1% of the time, Pallas kernels for 0%

commit v1 on v0

v1 whole, which is shorter than its diff:
```python
import math

import jax
import jax.numpy as jnp
from jax import lax
from jax.experimental import pallas as pl
from jax.experimental.pallas import tpu as pltpu
from jax.sharding import PartitionSpec as P

stiff_floor = 0.001
damping = 0.6
coarse_damping = 0.5

MESH = pl.DeviceIdType.MESH
AXES = ("gx", "gy", "gz")
GROUPS = (24, 4, 8)
EDGE = 1.0
FACE = 2.0 - math.sqrt(2.0)
CORNER = 2.0 - math.sqrt(3.0)

LAME = 0.3 / (1.3 * 0.4)
SHEAR = 0.5 / 1.3
NORMAL = (LAME + 2.0 * SHEAR) / 16.0
CROSS = LAME / 16.0
TWIST = SHEAR / 16.0
BEND = (LAME + 2.0 * SHEAR + SHEAR) / 48.0
BEND_CROSS = LAME / 48.0
SPIN = SHEAR / 48.0
HOUR = (LAME + 2.0 * SHEAR + 2.0 * SHEAR) / 144.0
NODE_DIAG = (LAME + 2.0 * SHEAR + 2.0 * SHEAR) / 9.0

YZ = [(j, k) for j in (-1, 0, 1) for k in (-1, 0, 1) if (j, k) != (0, 0)]


def device(dx, dy, dz):
    return tuple(
        lax.rem(lax.axis_index(axis) + (step + count), count)
        for axis, step, count in zip(AXES, (dx, dy, dz), GROUPS)
    )


def partner():
    place = lax.axis_index("gx")
    return (place + 1 - 2 * lax.rem(place, 2), lax.axis_index("gy"), lax.axis_index("gz"))


def zp(v):
    return pltpu.roll(v, v.shape[1] - 1, 1)


def zm(v):
    return pltpu.roll(v, 1, 1)


def yp(v):
    return pltpu.roll(v, v.shape[0] - 1, 0)


def ym(v):
    return pltpu.roll(v, 1, 0)


def forward(field):
    modes = {}
    for c in range(3):
        u = field[c]
        up = zp(u)
        for r, w in ((0, u + up), (1, up - u)):
            wp = yp(w)
            modes[c, 0, r] = w + wp
            modes[c, 1, r] = wp - w
    return modes


def across(low, high):
    modes = {}
    for (c, q, r), a in low.items():
        b = high[c, q, r]
        if (q, r) != (0, 0):
            modes[c, 0, q, r] = a + b
        modes[c, 1, q, r] = b - a
    return modes


def stress(u):
    f = {}
    total = (u[0, 1, 0, 0] + u[1, 0, 1, 0] + u[2, 0, 0, 1]) * CROSS
    for c, mode in ((0, (1, 0, 0)), (1, (0, 1, 0)), (2, (0, 0, 1))):
        f[(c,) + mode] = u[(c,) + mode] * (NORMAL - CROSS) + total
    for a, b in (
        ((0, 0, 0, 1), (2, 1, 0, 0)),
        ((0, 0, 1, 0), (1, 1, 0, 0)),
        ((1, 0, 0, 1), (2, 0, 1, 0)),
    ):
        f[a] = f[b] = (u[a] + u[b]) * TWIST
    total = u[0, 0, 1, 1] + u[1, 1, 0, 1] + u[2, 1, 1, 0]
    for a in ((0, 0, 1, 1), (1, 1, 0, 1), (2, 1, 1, 0)):
        f[a] = (u[a] + total) * SPIN
    for a, b in (
        ((0, 1, 0, 1), (1, 0, 1, 1)),
        ((0, 1, 1, 0), (2, 0, 1, 1)),
        ((1, 1, 1, 0), (2, 1, 0, 1)),
    ):
        f[a] = u[a] * BEND + u[b] * BEND_CROSS
        f[b] = u[b] * BEND + u[a] * BEND_CROSS
    for c in range(3):
        f[c, 1, 1, 1] = u[c, 1, 1, 1] * HOUR
    return f


def scaled(f, factor):
    out, seen = {}, {}
    for mode, value in f.items():
        if id(value) not in seen:
            seen[id(value)] = value * factor
        out[mode] = seen[id(value)]
    return out


def backward(modes):
    rows = []
    for c in range(3):
        lines = []
        for r in (0, 1):
            s, d = modes[c, 0, r], modes[c, 1, r]
            lines.append((s - d) + ym(s + d))
        rows.append((lines[0] - lines[1]) + zm(lines[0] + lines[1]))
    return rows


def stiffness_product(nodes, factors):
    count = len(nodes)
    result, carry = [], None
    low = forward(nodes[0])
    for e in range(count - 1):
        high = forward(nodes[e + 1])
        f = scaled(stress(across(low, high)), factors[e])
        here, later = {}, {}
        for c, q, r in low:
            d = f[c, 1, q, r]
            if (q, r) == (0, 0):
                here[c, q, r] = -d
                later[c, q, r] = d
            else:
                s = f[c, 0, q, r]
                here[c, q, r] = s - d
                later[c, q, r] = s + d
        if carry is not None:
            result.append(backward({mode: carry[mode] + here[mode] for mode in here}))
        carry, low = later, high
    return result


def operator(planes, factors, free):
    held = [[free[p] * planes[p][c] for c in range(3)] for p in range(len(planes))]
    forces = stiffness_product(held, factors)
    return [
        [
            free[p] * forces[p - 1][c] + (planes[p][c] - held[p][c])
            for c in range(3)
        ]
        for p in range(1, len(planes) - 1)
    ]


def smooth_plane(v):
    along_z = zp(v) + zm(v)
    along_y = yp(v) + ym(v)
    both = yp(along_z) + ym(along_z)
    sides = along_z + along_y
    return 2.0 * v + EDGE * sides + FACE * both, EDGE * v + FACE * sides + CORNER * both


def smooth(planes):
    parts = [smooth_plane(v) for v in planes]
    return [
        parts[p][0] + (parts[p - 1][1] + parts[p + 1][1]) for p in range(1, len(planes) - 1)
    ]


def block_sum(low, high, even_y, even_z):
    v = low + high
    v = v + jnp.where(even_z, zp(v), zm(v))
    return v + jnp.where(even_y, yp(v), ym(v))


def iota(shape, dim):
    return lax.broadcasted_iota(jnp.int32, shape, dim)


def pack(tiles):
    slot = iota((8, 128), 1) >> 3
    packs = []
    for first in range(0, len(tiles), 16):
        total = None
        for s, tile in enumerate(tiles[first : first + 16]):
            turned = pltpu.roll(tile, (4 + 8 * s) % 128, 1)
            total = turned if total is None else jnp.where(slot == s, turned, total)
        packs.append(total)
    return packs


def unpack(packed, s):
    return pltpu.roll(packed, (124 - 8 * (s % 16)) % 128, 1)


def kernel(
    design_hbm, passive_hbm, fixed_hbm, state_hbm, adjoint_hbm, resid_hbm,
    adjoint_out, resid_out, grad_out,
    design, passive, fixed, own_sa, in_sem,
    own0, z0, ly0, lz0, lc0, em0, er0, ea0, xm0, xf0, xr0, xa0,
    z2, ly2, lz2, lc2, e2, x2,
    own1, z1, ly1, lz1, lc1, e1, x1,
    own3, z3, ly3, lz3, lc3, e3, x3,
    ar_send, ar_land, send_sem, recv_sem,
):
    copies = []

    def send(src, dst, target):
        number = len(copies)
        copy = pltpu.make_async_remote_copy(
            src_ref=src,
            dst_ref=dst,
            send_sem=send_sem.at[number],
            recv_sem=recv_sem.at[number],
            device_id=target,
            device_id_type=MESH,
        )
        copy.start()
        copies.append(copy)
        return copy

    def arrive(group):
        for copy in group:
            copy.wait_recv()

    barrier = pltpu.get_barrier_semaphore()
    friends = [(0, j, k) for j, k in YZ] + [(1, 0, 0), (-1, 0, 0)]
    friends += [(2 * i, 0, 0) for i in range(1, 12)] + [(0, 2, 0)] + [(0, 0, k) for k in range(2, 7)]
    for friend in friends:
        pl.semaphore_signal(barrier, inc=1, device_id=device(*friend), device_id_type=MESH)

    inputs = [
        pltpu.make_async_copy(src, dst, in_sem.at[n])
        for n, (src, dst) in enumerate(
            (
                (design_hbm, design),
                (passive_hbm, passive),
                (fixed_hbm, fixed),
                (resid_hbm, own0.at[pl.ds(8, 12)]),
                (adjoint_hbm, own_sa.at[pl.ds(0, 12)]),
                (state_hbm, own_sa.at[pl.ds(12, 12)]),
            )
        )
    ]
    for copy in inputs:
        copy.start()

    place_x, place_y, place_z = (lax.axis_index(axis) for axis in AXES)
    wide = (16, 256)
    row, lane = iota(wide, 0), iota(wide, 1)
    at_y = place_y * 8 + jnp.where(row < 12, row, row - 16)
    at_z = place_z * 128 + jnp.where(lane < 192, lane, lane - 256)
    inside = ((at_y >= 0) & (at_y < 32) & (at_z >= 0) & (at_z < 1024)).astype(jnp.float32)
    inside_low = inside * (place_x > 0).astype(jnp.float32)
    inside_high = inside * (place_x < 23).astype(jnp.float32)

    def sides(dim_at, count):
        return (dim_at > 0).astype(jnp.float32) + (dim_at < count - 1).astype(jnp.float32)

    near_y, near_z = sides(at_y, 32), sides(at_z, 1024)
    near, nearer = near_y + near_z, near_y * near_z
    weight_base = 2.0 + EDGE * near + FACE * nearer
    weight_step = EDGE + FACE * near + CORNER * nearer
    inverse_inner = 1.0 / (weight_base + 2.0 * weight_step)
    inverse_end = 1.0 / (weight_base + weight_step)
    inverse_first = jnp.where(place_x > 0, inverse_inner, inverse_end)
    inverse_last = jnp.where(place_x < 23, inverse_inner, inverse_end)

    def inverse_weight(p):
        return inverse_first if p == 0 else inverse_last if p == 3 else inverse_inner

    even_y, even_z = (row & 1) == 0, (lane & 1) == 0
    tile_even_y, tile_even_z = (iota((8, 128), 0) & 1) == 0, (iota((8, 128), 1) & 1) == 0
    top_half = iota((8, 128), 0) < 4
    low_slot = (iota((8, 128), 1) & 7) < 4

    for copy in inputs[:3]:
        copy.wait()
    own0[0:4] = jnp.where(passive[...] == 1, 0.0, jnp.where(passive[...] == 2, 1.0, design[...]))
    own0[4:8] = (1 - fixed[...]).astype(jnp.float32)
    inputs[3].wait()
    for n, packed in enumerate(pack([own0[t] for t in range(20)])):
        z0[n] = packed
    pl.semaphore_wait(barrier, len(friends))

    def flat_sends(own, edges, land_y, land_z, land_c):
        group = {}
        for n, (j, k) in enumerate((j, k) for j in (-1, 1) for k in (-1, 1)):
            group[j, k] = send(edges, land_c.at[n], device(0, j, k))
        for n, k in enumerate((-1, 1)):
            group[0, k] = send(edges, land_z.at[n], device(0, 0, k))
        for n, j in enumerate((-1, 1)):
            group[j, 0] = send(own, land_y.at[n], device(0, j, 0))
        return group.values()

    def rows_beside(land_y, t):
        return jnp.where(top_half, land_y[0, t], land_y[1, t])

    def edges_beside(land_z, land_c, n):
        top = jnp.where(low_slot, land_z[1, n], land_z[0, n])
        from_low_y = jnp.where(low_slot, land_c[3, n], land_c[2, n])
        from_high_y = jnp.where(low_slot, land_c[1, n], land_c[0, n])
        return jnp.concatenate([top, jnp.where(top_half, from_high_y, from_low_y)], 0)

    def widened(main, packed, s):
        return jnp.concatenate([main, unpack(packed, s)], 1)

    arrive(flat_sends(own0, z0, ly0, lz0, lc0))
    edges0 = [edges_beside(lz0, lc0, n) for n in range(2)]
    mains = [jnp.concatenate([own0[t], rows_beside(ly0, t)], 0) for t in range(20)]
    for t in range(8):
        em0[t] = mains[t]
    for t in range(12):
        er0[t // 4, t % 4] = mains[8 + t]
    for n in range(2):
        ea0[n] = edges0[n]
    group = [
        send(em0.at[pl.ds(0, 3)], xm0.at[0, pl.ds(0, 3)], device(-1, 0, 0)),
        send(em0.at[pl.ds(4, 3)], xf0.at[0], device(-1, 0, 0)),
        send(er0.at[:, pl.ds(0, 2)], xr0.at[0], device(-1, 0, 0)),
        send(ea0, xa0.at[0], device(-1, 0, 0)),
        send(em0.at[pl.ds(0, 4)], xm0.at[1], device(1, 0, 0)),
        send(em0.at[pl.ds(5, 3)], xf0.at[1], device(1, 0, 0)),
        send(er0.at[:, pl.ds(2, 2)], xr0.at[1], device(1, 0, 0)),
        send(ea0, xa0.at[1], device(1, 0, 0)),
    ]

    inputs[4].wait()
    inputs[5].wait()
    for n, packed in enumerate(pack([own_sa[t] for t in range(24)])):
        z2[n] = packed
    group2 = [
        send(own_sa, ly2, device(0, -1, 0)),
        send(z2, lz2, device(0, 0, -1)),
        send(z2, lc2, device(0, -1, -1)),
    ]

    arrive(group)
    masked = [widened(xm0[1, p], xa0[1, 0], p) * inside_low for p in range(4)]
    masked += [widened(mains[p], edges0[0], p) * inside for p in range(4)]
    masked += [widened(xm0[0, p], xa0[0, 0], p) * inside_high for p in range(3)]
    free = [widened(xf0[1, p], xa0[1, 0], 5 + p) * inside_low for p in range(3)]
    free += [widened(mains[4 + p], edges0[0], 4 + p) * inside for p in range(4)]
    free += [widened(xf0[0, p], xa0[0, 0], 4 + p) * inside_high for p in range(3)]
    resid = [
        [widened(xr0[1, c, p], xa0[1, (10 + 4 * c + p) // 16], 10 + 4 * c + p) * inside_low for c in range(3)]
        for p in range(2)
    ]
    resid += [
        [widened(mains[8 + 4 * c + p], edges0[(8 + 4 * c + p) // 16], 8 + 4 * c + p) * inside for c in range(3)]
        for p in range(4)
    ]
    resid += [
        [widened(xr0[0, c, p], xa0[0, (8 + 4 * c + p) // 16], 8 + 4 * c + p) * inside_high for c in range(3)]
        for p in range(2)
    ]

    smoothed = smooth(masked)
    density, factor = {}, {}
    for p in range(-3, 6):
        inverse = inverse_weight(p) if 0 <= p < 4 else inverse_inner
        if p == -1 or p == 4:
            inverse = inverse_inner
        if p == -3:
            inverse = inverse_inner
        density[p] = smoothed[p + 3] * inverse
    for p in range(-3, 6):
        edge = inside_low if p < 0 else inside if p < 4 else inside_high
        d = density[p]
        factor[p] = edge * (stiff_floor + d * d * d * (1.0 - stiff_floor))

    paired = {}
    for p in range(-3, 6):
        v = factor[p] + zm(factor[p])
        paired[p] = v + ym(v)
    free = {p: free[p + 3] for p in range(-3, 7)}
    resid = {p: resid[p + 2] for p in range(-2, 6)}
    diagonal, inverse_diag, first = {}, {}, {}
    for p in range(-2, 6):
        diagonal[p] = free[p] * (NODE_DIAG * (paired[p] + paired[p - 1])) + (1.0 - free[p])
        inverse_diag[p] = 1.0 / diagonal[p]
        first[p] = [damping * resid[p][c] * inverse_diag[p] for c in range(3)]

    def apply(field, lowest, highest):
        span = range(lowest - 1, highest + 2)
        result = operator(
            [field[p] for p in span],
            [factor[p] for p in range(lowest - 1, highest + 1)],
            [free[p] for p in span],
        )
        return {p: result[p - lowest] for p in range(lowest, highest + 1)}

    image = apply(first, 0, 3)
    second = [
        [(resid[p][c] - image[p][c])[0:8, 0:128] for c in range(3)] for p in range(4)
    ]
    coarse_diag = [
        block_sum(diagonal[2 * k], diagonal[2 * k + 1], even_y, even_z) for k in range(-1, 3)
    ]
    inverse_coarse = [1.0 / d for d in coarse_diag]
    coarse_own = []
    for c in range(3):
        for k in range(2):
            total = block_sum(second[2 * k][c], second[2 * k + 1][c], tile_even_y, tile_even_z)
            coarse_own.append(coarse_damping * total * inverse_coarse[k + 1][0:8, 0:128])
    for t in range(6):
        own1[t] = coarse_own[t]
    z1[0] = pack(coarse_own)[0]
    group = flat_sends(own1, z1, ly1, lz1, lc1)

    arrive(group2)
    edges2 = []
    for n in range(2):
        edges2.append(jnp.concatenate([lz2[n], lc2[n]], 0))
        e2[6 + n] = edges2[n]
    mains2 = [jnp.concatenate([own_sa[t], ly2[t]], 0) for t in range(24)]
    for f in range(6):
        e2[f] = mains2[4 * f]

    arrive(group)
    edges1 = edges_beside(lz1, lc1, 0)
    mains1 = [jnp.concatenate([coarse_own[t], rows_beside(ly1, t)], 0) for t in range(6)]
    for t in range(6):
        e1[t] = mains1[t]
    e1[6] = edges1
    group = [
        send(e1, x1.at[0], device(-1, 0, 0)),
        send(e1, x1.at[1], device(1, 0, 0)),
    ]
    group2 = [send(e2, x2, device(-1, 0, 0))]
    arrive(group)
    coarse = {}
    for k in range(2):
        coarse[k - 2] = [widened(x1[1, 2 * c + k], x1[1, 6], 2 * c + k) * inside_low for c in range(3)]
        coarse[k] = [widened(mains1[2 * c + k], edges1, 2 * c + k) * inside for c in range(3)]
        coarse[k + 2] = [widened(x1[0, 2 * c + k], x1[0, 6], 2 * c + k) * inside_high for c in range(3)]
    spread = {p: coarse[p // 2] for p in range(-4, 8)}
    image = apply(spread, -2, 5)
    middle = {}
    for k in range(-1, 3):
        for c in range(3):
            total = block_sum(image[2 * k][c], image[2 * k + 1][c], even_y, even_z)
            fix = 2.0 * coarse[k][c] - coarse_damping * total * inverse_coarse[k + 1]
            for p in (2 * k, 2 * k + 1):
                middle.setdefault(p, []).append(first[p][c] + fix)
    image = apply(middle, -1, 4)
    direction = {
        p: [
            middle[p][c] + damping * (resid[p][c] - image[p][c]) * inverse_diag[p]
            for c in range(3)
        ]
        for p in range(-1, 5)
    }
    image = apply(direction, 0, 3)
    image = {p: [image[p][c][0:8, 0:128] for c in range(3)] for p in range(4)}
    numerator = denominator = None
    for p in range(4):
        for c in range(3):
            d = direction[p][c][0:8, 0:128]
            a, b = resid[p][c][0:8, 0:128] * d, d * image[p][c]
            numerator = a if numerator is None else numerator + a
            denominator = b if denominator is None else denominator + b
    numerator = numerator + pltpu.roll(numerator, 4, 0)
    denominator = denominator + pltpu.roll(denominator, 4, 0)
    sums = jnp.where(top_half, numerator, denominator)

    landed = [0]

    def spread_sums(stage, value, targets):
        ar_send[stage] = value
        base = landed[0]
        landed[0] += len(targets)
        group = [
            send(ar_send.at[stage], ar_land.at[base + n], target)
            for n, target in enumerate(targets)
        ]

        def gather():
            arrive(group)
            total = value
            for n in range(len(targets)):
                total = total + ar_land[base + n]
            return total

        return gather

    sums = spread_sums(0, sums, [partner()])()
    gather = spread_sums(1, sums, [device(2 * i, 0, 0) for i in (6, 5, 7, 4, 8, 3, 9, 2, 10, 1, 11)])

    arrive(group2)
    def ends(f, p):
        if p < 4:
            return widened(mains2[4 * f + p], edges2[(4 * f + p) // 16], 4 * f + p) * inside
        return widened(x2[f], x2[6 + (4 * f) // 16], 4 * f) * inside_high

    def corner_modes(fields):
        return [{m: v[0:8, 0:128] for m, v in forward(fields[p]).items()} for p in range(5)]

    adjoint_modes = corner_modes([[ends(c, p) for c in range(3)] for p in range(5)])
    state_modes = corner_modes([[ends(3 + c, p) for c in range(3)] for p in range(5)])
    direction_modes = corner_modes([direction[p] for p in range(5)])
    sens = []
    for p in range(4):
        force = stress(across(state_modes[p], state_modes[p + 1]))
        d = density[p][0:8, 0:128]
        weight = 3.0 * (1.0 - stiff_floor) * d * d * inverse_weight(p)[0:8, 0:128]
        for modes in (adjoint_modes, direction_modes):
            with_modes = across(modes[p], modes[p + 1])
            energy = None
            for mode, value in force.items():
                term = with_modes[mode] * value
                energy = term if energy is None else energy + term
            sens.append(weight * energy)
    for t in range(8):
        own3[t] = sens[t]
    z3[0] = pack(sens)[0]
    group = flat_sends(own3, z3, ly3, lz3, lc3)
    sums = gather()
    gather = spread_sums(2, sums, [device(0, 0, k) for k in (4, 3, 5, 2, 6, 1, 7)])
    arrive(group)
    edges3 = edges_beside(lz3, lc3, 0)
    mains3 = [jnp.concatenate([sens[t], rows_beside(ly3, t)], 0) for t in range(8)]
    e3[0] = mains3[0]
    e3[1] = mains3[1]
    e3[2] = edges3
    e3[3] = mains3[6]
    e3[4] = mains3[7]
    group = [
        send(e3.at[pl.ds(0, 3)], x3.at[0], device(-1, 0, 0)),
        send(e3.at[pl.ds(2, 3)], x3.at[1], device(1, 0, 0)),
    ]
    sums = gather()
    gather = spread_sums(3, sums, [device(0, j, 0) for j in (2, 1, 3)])
    arrive(group)
    grads = []
    for f in range(2):
        planes = [widened(x3[1, 1 + f], x3[1, 0], 6 + f) * inside_low]
        planes += [widened(mains3[2 * p + f], edges3, 2 * p + f) * inside for p in range(4)]
        planes += [widened(x3[0, f], x3[0, 2], f) * inside_high]
        grads.append([v[0:8, 0:128] for v in smooth(planes)])
    sums = gather()
    numerator = jnp.sum(jnp.where(top_half, sums, 0.0), axis=(0, 1), keepdims=True)
    denominator = jnp.sum(jnp.where(top_half, 0.0, sums), axis=(0, 1), keepdims=True)
    step = jnp.broadcast_to(numerator / denominator, (8, 128))
    for p in range(4):
        for c in range(3):
            adjoint_out[c, p] = own_sa[4 * c + p] + step * direction[p][c][0:8, 0:128]
            resid_out[c, p] = own0[8 + 4 * c + p] - step * image[p][c]
        grad_out[p] = jnp.where(passive[p] == 0, grads[0][p] + step * grads[1][p], 0.0)
    for copy in copies:
        copy.wait_send()


def body(design, passive, fixed, state, adjoint, resid):
    def scratch(*shape):
        return pltpu.VMEM(shape, jnp.float32)

    n_copies = 8 + 8 + 3 + 8 + 2 + 1 + 22 + 8 + 2
    return pl.pallas_call(
        kernel,
        out_shape=(
            jax.ShapeDtypeStruct((3, 4, 8, 128), jnp.float32),
            jax.ShapeDtypeStruct((3, 4, 8, 128), jnp.float32),
            jax.ShapeDtypeStruct((4, 8, 128), jnp.float32),
        ),
        in_specs=[pl.BlockSpec(memory_space=pl.ANY)] * 6,
        out_specs=(pl.BlockSpec(memory_space=pltpu.VMEM),) * 3,
        scratch_shapes=[
            scratch(4, 8, 128),
            pltpu.VMEM((4, 8, 128), jnp.int32),
            pltpu.VMEM((4, 8, 128), jnp.int32),
            scratch(24, 8, 128),
            pltpu.SemaphoreType.DMA((6,)),
            scratch(20, 8, 128),
            scratch(2, 8, 128),
            scratch(2, 20, 8, 128),
            scratch(2, 2, 8, 128),
            scratch(4, 2, 8, 128),
            scratch(8, 16, 128),
            scratch(3, 4, 16, 128),
            scratch(2, 16, 128),
            scratch(2, 4, 16, 128),
            scratch(2, 3, 16, 128),
            scratch(2, 3, 2, 16, 128),
            scratch(2, 2, 16, 128),
            scratch(2, 8, 128),
            scratch(24, 8, 128),
            scratch(2, 8, 128),
            scratch(2, 8, 128),
            scratch(8, 16, 128),
            scratch(8, 16, 128),
            scratch(6, 8, 128),
            scratch(1, 8, 128),
            scratch(2, 6, 8, 128),
            scratch(2, 1, 8, 128),
            scratch(4, 1, 8, 128),
            scratch(7, 16, 128),
            scratch(2, 7, 16, 128),
            scratch(8, 8, 128),
            scratch(1, 8, 128),
            scratch(2, 8, 8, 128),
            scratch(2, 1, 8, 128),
            scratch(4, 1, 8, 128),
            scratch(5, 16, 128),
            scratch(2, 3, 16, 128),
            scratch(4, 8, 128),
            scratch(22, 8, 128),
            pltpu.SemaphoreType.DMA((n_copies,)),
            pltpu.SemaphoreType.DMA((n_copies,)),
        ],
        compiler_params=pltpu.CompilerParams(
            collective_id=0, has_side_effects=True, vmem_limit_bytes=32 * 2**20
        ),
    )(
        design,
        passive,
        fixed,
        state.reshape(12, 8, 128),
        adjoint.reshape(12, 8, 128),
        resid.reshape(12, 8, 128),
    )


def solution(mesh):
    return jax.shard_map(
        body,
        mesh=mesh,
        in_specs=(P("gx", "gy", "gz"),) * 3 + (P(None, "gx", "gy", "gz"),) * 3,
        out_specs=(P(None, "gx", "gy", "gz"), P(None, "gx", "gy", "gz"), P("gx", "gy", "gz")),
        check_vma=False,
    )
```

time: 334 us -> 61.1 us (0.18); the launches traced: 329 us -> 60.7 us
  blocking collectives: 111 us -> 0 us
  starting transfers between devices: 93.6 us -> 0 us
  waiting for transfers between devices: 71.3 us -> 0 us
  Pallas kernels: 0 us -> 53.6 us
  other arithmetic: 22 us -> 0 us
  local copies, waits for them, and re-layouts: 23.9 us -> 6.38 us
  matrix products: 3.88 us -> 0 us
    psum x1 -> x0, blocking collectives: 111 us -> none  [body(): numerator = lax.psum(jnp.sum(resid * direction), ('gx', 'gy', 'gz'))]
    ppermute x36 -> x0, starting transfers between devices: 93.6 us -> none  [the longest x18 59.1 us: extended(): lax.ppermute(tail, axis, [(i, (i + 1) % count) for i in range(ends)])]
    ppermute x36 -> x0, waiting for transfers between devices: 71.3 us -> none  [the longest x18 57.4 us: extended(): lax.ppermute(head, axis, [((i + 1) % count, i) for i in range(ends)])]
    pallas_call x0 -> x1, Pallas kernels: none -> 53.6 us  [body(): pl.pallas_call(kernel, out_shape=(jax.ShapeDtypeStruct((3, 4, 8, 128), jn...]
    reshape x19 -> x0, local copies, waits for them, and re-layouts: 11.7 us -> none  [the longest x2 7.77 us: restrict(): field.reshape(3, shape[1] // 2, 2, shape[2] // 2, 2, shape[3] // 2, 2)]
    add x9 -> x0, other arithmetic: 8.53 us -> none  [the longest x2 5.21 us: flat_stencil(): total = total + weight * flat[:, offset:offset + usable]]
    dot_general x5 -> x0, matrix products: 3.88 us -> none  [the longest x4 2.64 us: element_forces(): jnp.dot(stiffness, gathered, precision=lax.Precision.HIGHEST)]
    concatenate x13 -> x0, other arithmetic: 3.68 us -> none  [the longest x12 2.87 us: extended(): jnp.concatenate([lax.ppermute(tail, axis, [(i, (i + 1) % count) for i in...]
  transfers between devices with their start and end apart: 36 -> 0, of which waited for: 24 -> 0; matrix products, arithmetic and copies ran while one was open for 1% -> 0% of each run, Pallas kernels for 0% -> 0%
where the time goes in v1:
time: 61.1 us; the launch traced here: 60.7 us
  Pallas kernels  53.6 us (88%)
  local copies, waits for them, and re-layouts  6.38 us (10%)
  between operations  0.65 us (1%)
    pallas_call x1, Pallas kernels, body(): pl.pallas_call(kernel, out_shape=(jax.ShapeDtypeStruct((3, 4, 8, 128), jn...  53.6 us
    unnamed x15, local copies, waits for them, and re-layouts  6.38 us

profile of v1, /device:TPU:1, one launch (start us, length us, event | category | flops | bytes accessed | tf_op | source)
XLA Modules:
  0.0 60.7 jit_solution(4737713669738160490)
XLA Ops:
  0.6 0.0 copy-start
  0.6 0.8 %copy-done = f32[3,4,8,128]{3,2,1,0:T(8,128)S(1)} copy-done((f32[3,4,8,128]{3,2,1,0:T(8,128)S(1)}, f32[3,4,8,128]{3,2,1,0:T(8,128)}, u32[]{:S(2)}) %copy-start) | copy-done | bytes 49176
  1.4 0.0 copy-start.1
  1.4 0.8 %copy-done.1 = f32[3,4,8,128]{3,2,1,0:T(8,128)S(1)} copy-done((f32[3,4,8,128]{3,2,1,0:T(8,128)S(1)}, f32[3,4,8,128]{3,2,1,0:T(8,128)}, u32[]{:S(2)}) %copy-start.1) | copy-done | bytes 49176
  2.2 0.0 copy-start.2
  2.2 0.8 %copy-done.2 = f32[3,4,8,128]{3,2,1,0:T(8,128)S(1)} copy-done((f32[3,4,8,128]{3,2,1,0:T(8,128)S(1)}, f32[3,4,8,128]{3,2,1,0:T(8,128)}, u32[]{:S(2)}) %copy-start.2) | copy-done | bytes 49176
  3.0 0.0 copy-start.3
  3.0 0.7 %copy-done.3 = f32[4,8,128]{2,1,0:T(8,128)S(1)} copy-done((f32[4,8,128]{2,1,0:T(8,128)S(1)}, f32[4,8,128]{2,1,0:T(8,128)}, u32[]{:S(2)}) %copy-start.3) | copy-done | bytes 16408
  3.7 0.0 copy-start.4
  3.7 0.7 %copy-done.4 = s32[4,8,128]{2,1,0:T(8,128)S(1)} copy-done((s32[4,8,128]{2,1,0:T(8,128)S(1)}, s32[4,8,128]{2,1,0:T(8,128)}, u32[]{:S(2)}) %copy-start.4) | copy-done | bytes 16408
  4.5 0.0 copy-start.5
  4.5 0.7 %copy-done.5 = s32[4,8,128]{2,1,0:T(8,128)S(1)} copy-done((s32[4,8,128]{2,1,0:T(8,128)S(1)}, s32[4,8,128]{2,1,0:T(8,128)}, u32[]{:S(2)}) %copy-start.5) | copy-done | bytes 16408
  5.2 53.6 %shard_map.85 = (f32[3,4,8,128]{3,2,1,0:T(8,128)S(1)}, f32[3,4,8,128]{3,2,1,0:T(8,128)S(1)}, f32[4,8,128]{2,1,0:T(8,128)S(1)}) custom-call(f32[4,8,128]{2,1,0:T(8,128)S(1)} %copy-done.3, s32[4,8,128]{2,1,0:T(8,128)S(1)} %copy-done.4, s32[4,8,128]{2,1,0:T(8,128)S(1)} %copy-done.5, f32[12,8,128]{2,1,0:T(8,128)S(1)} %bitcast.3, f32[12,8,128]{2,1,0:T(8,128)S(1)} %bitcast.4, ...), custom_call_target="tpu_custom_call" | custom-call | tf_op jit(solution)/shard_map/pallas_call | solution.py:570
  58.8 0.6 %copy.12 = f32[3,4,8,128]{3,2,1,0:T(8,128)} copy(f32[3,4,8,128]{3,2,1,0:T(8,128)S(1)} %get-tuple-element.6) | data formatting | bytes 98304
  59.4 0.6 %copy.13 = f32[3,4,8,128]{3,2,1,0:T(8,128)} copy(f32[3,4,8,128]{3,2,1,0:T(8,128)S(1)} %get-tuple-element.7) | data formatting | bytes 98304
  60.1 0.6 copy.14
Async XLA Ops:
  0.6 0.8 %copy-start = (f32[3,4,8,128]{3,2,1,0:T(8,128)S(1)}, f32[3,4,8,128]{3,2,1,0:T(8,128)}, u32[]{:S(2)}) copy-start(f32[3,4,8,128]{3,2,1,0:T(8,128)} %param.9) | copy-start | bytes 147460
  1.4 0.8 %copy-start.1 = (f32[3,4,8,128]{3,2,1,0:T(8,128)S(1)}, f32[3,4,8,128]{3,2,1,0:T(8,128)}, u32[]{:S(2)}) copy-start(f32[3,4,8,128]{3,2,1,0:T(8,128)} %param.10) | copy-start | bytes 147460
  2.2 0.8 %copy-start.2 = (f32[3,4,8,128]{3,2,1,0:T(8,128)S(1)}, f32[3,4,8,128]{3,2,1,0:T(8,128)}, u32[]{:S(2)}) copy-start(f32[3,4,8,128]{3,2,1,0:T(8,128)} %param.11) | copy-start | bytes 147460
  3.0 0.7 %copy-start.3 = (f32[4,8,128]{2,1,0:T(8,128)S(1)}, f32[4,8,128]{2,1,0:T(8,128)}, u32[]{:S(2)}) copy-start(f32[4,8,128]{2,1,0:T(8,128)} %design_hbm.1) | copy-start | bytes 49156
  3.7 0.7 %copy-start.4 = (s32[4,8,128]{2,1,0:T(8,128)S(1)}, s32[4,8,128]{2,1,0:T(8,128)}, u32[]{:S(2)}) copy-start(s32[4,8,128]{2,1,0:T(8,128)} %passive_hbm.1) | copy-start | bytes 49156
  4.5 0.7 %copy-start.5 = (s32[4,8,128]{2,1,0:T(8,128)S(1)}, s32[4,8,128]{2,1,0:T(8,128)}, u32[]{:S(2)}) copy-start(s32[4,8,128]{2,1,0:T(8,128)} %fixed_hbm.1) | copy-start | bytes 49156

commit v2 on v1

--- a/solution.py
+++ b/solution.py
@@ -236,7 +236,7 @@
 
     barrier = pltpu.get_barrier_semaphore()
     friends = [(0, j, k) for j, k in YZ] + [(1, 0, 0), (-1, 0, 0)]
-    friends += [(2 * i, 0, 0) for i in range(1, 12)] + [(0, 2, 0)] + [(0, 0, k) for k in range(2, 7)]
+    friends += [(2 * i, 0, 0) for i in (1, -1, 2, -2)]
     for friend in friends:
         pl.semaphore_signal(barrier, inc=1, device_id=device(*friend), device_id_type=MESH)
 
@@ -301,11 +301,12 @@
         for n, k in enumerate((-1, 1)):
             group[0, k] = send(edges, land_z.at[n], device(0, 0, k))
         for n, j in enumerate((-1, 1)):
-            group[j, 0] = send(own, land_y.at[n], device(0, j, 0))
+            half = pl.ds(4 * n, 4)
+            group[j, 0] = send(own.at[:, half], land_y.at[:, half], device(0, j, 0))
         return group.values()
 
     def rows_beside(land_y, t):
-        return jnp.where(top_half, land_y[0, t], land_y[1, t])
+        return land_y[t]
 
     def edges_beside(land_z, land_c, n):
         top = jnp.where(low_slot, land_z[1, n], land_z[0, n])
@@ -341,7 +342,7 @@
     for n, packed in enumerate(pack([own_sa[t] for t in range(24)])):
         z2[n] = packed
     group2 = [
-        send(own_sa, ly2, device(0, -1, 0)),
+        send(own_sa.at[:, pl.ds(0, 1)], ly2.at[:, pl.ds(0, 1)], device(0, -1, 0)),
         send(z2, lz2, device(0, 0, -1)),
         send(z2, lc2, device(0, -1, -1)),
     ]
@@ -496,8 +497,7 @@
         return gather
 
     sums = spread_sums(0, sums, [partner()])()
-    gather = spread_sums(1, sums, [device(2 * i, 0, 0) for i in (6, 5, 7, 4, 8, 3, 9, 2, 10, 1, 11)])
-
+    gather = spread_sums(1, sums, [device(2 * i, 0, 0) for i in (2, 1, -1)])
     arrive(group2)
     def ends(f, p):
         if p < 4:
@@ -527,7 +527,7 @@
     z3[0] = pack(sens)[0]
     group = flat_sends(own3, z3, ly3, lz3, lc3)
     sums = gather()
-    gather = spread_sums(2, sums, [device(0, 0, k) for k in (4, 3, 5, 2, 6, 1, 7)])
+    gather = spread_sums(2, sums, [device(2 * i, 0, 0) for i in (4, -4)])
     arrive(group)
     edges3 = edges_beside(lz3, lc3, 0)
     mains3 = [jnp.concatenate([sens[t], rows_beside(ly3, t)], 0) for t in range(8)]
@@ -541,7 +541,7 @@
         send(e3.at[pl.ds(2, 3)], x3.at[1], device(1, 0, 0)),
     ]
     sums = gather()
-    gather = spread_sums(3, sums, [device(0, j, 0) for j in (2, 1, 3)])
+    gather = spread_sums(3, sums, [device(0, 0, k) for k in (4, 3, 5, 2, 6, 1, 7)])
     arrive(group)
     grads = []
     for f in range(2):
@@ -550,6 +550,7 @@
         planes += [widened(x3[0, f], x3[0, 2], f) * inside_high]
         grads.append([v[0:8, 0:128] for v in smooth(planes)])
     sums = gather()
+    sums = spread_sums(4, sums, [device(0, j, 0) for j in (2, 1, 3)])()
     numerator = jnp.sum(jnp.where(top_half, sums, 0.0), axis=(0, 1), keepdims=True)
     denominator = jnp.sum(jnp.where(top_half, 0.0, sums), axis=(0, 1), keepdims=True)
     step = jnp.broadcast_to(numerator / denominator, (8, 128))
@@ -566,7 +567,7 @@
     def scratch(*shape):
         return pltpu.VMEM(shape, jnp.float32)
 
-    n_copies = 8 + 8 + 3 + 8 + 2 + 1 + 22 + 8 + 2
+    n_copies = 8 + 8 + 3 + 8 + 2 + 1 + 16 + 8 + 2
     return pl.pallas_call(
         kernel,
         out_shape=(
@@ -584,7 +585,7 @@
             pltpu.SemaphoreType.DMA((6,)),
             scratch(20, 8, 128),
             scratch(2, 8, 128),
-            scratch(2, 20, 8, 128),
+            scratch(20, 8, 128),
             scratch(2, 2, 8, 128),
             scratch(4, 2, 8, 128),
             scratch(8, 16, 128),
@@ -602,25 +603,25 @@
             scratch(8, 16, 128),
             scratch(6, 8, 128),
             scratch(1, 8, 128),
-            scratch(2, 6, 8, 128),
+            scratch(6, 8, 128),
             scratch(2, 1, 8, 128),
             scratch(4, 1, 8, 128),
             scratch(7, 16, 128),
             scratch(2, 7, 16, 128),
             scratch(8, 8, 128),
             scratch(1, 8, 128),
-            scratch(2, 8, 8, 128),
+            scratch(8, 8, 128),
             scratch(2, 1, 8, 128),
             scratch(4, 1, 8, 128),
             scratch(5, 16, 128),
             scratch(2, 3, 16, 128),
-            scratch(4, 8, 128),
-            scratch(22, 8, 128),
+            scratch(5, 8, 128),
+            scratch(16, 8, 128),
             pltpu.SemaphoreType.DMA((n_copies,)),
             pltpu.SemaphoreType.DMA((n_copies,)),
         ],
         compiler_params=pltpu.CompilerParams(
-            collective_id=0, has_side_effects=True, vmem_limit_bytes=32 * 2**20
+            collective_id=0, has_side_effects=True, vmem_limit_bytes=62 * 2**20
         ),
     )(
         design,

time: 61.1 us -> 57.4 us (0.939)
  the two profiles are of different devices: /device:TPU:1 before, /device:TPU:2 now
where the time goes in v2:
time: 57.4 us; the launch traced here: 57.1 us
  Pallas kernels  53.7 us (94%)
  local copies, waits for them, and re-layouts  2.76 us (5%)
  between operations  0.65 us (1%)
    pallas_call x1, Pallas kernels, body(): pl.pallas_call(kernel, out_shape=(jax.ShapeDtypeStruct((3, 4, 8, 128), jn...  53.7 us
    unnamed x7, local copies, waits for them, and re-layouts  2.76 us

profile of v2, /device:TPU:2, one launch (start us, length us, event | category | flops | bytes accessed | tf_op | source)
XLA Modules:
  0.0 57.1 jit_solution(3033816980264752829)
XLA Ops:
  0.6 53.7 %shard_map.85 = (f32[3,4,8,128]{3,2,1,0:T(8,128)}, f32[3,4,8,128]{3,2,1,0:T(8,128)}, f32[4,8,128]{2,1,0:T(8,128)}) custom-call(f32[4,8,128]{2,1,0:T(8,128)} %design_hbm.1, s32[4,8,128]{2,1,0:T(8,128)} %passive_hbm.1, s32[4,8,128]{2,1,0:T(8,128)} %fixed_hbm.1, f32[12,8,128]{2,1,0:T(8,128)} %bitcast.3, f32[12,8,128]{2,1,0:T(8,128)} %bitcast.4, ...), custom_call_target="tpu_custom_call" | custom-call | tf_op jit(solution)/shard_map/pallas_call | solution.py:571
  54.3 0.0 copy-start
  54.3 1.4 %copy.12 = f32[3,4,8,128]{3,2,1,0:T(8,128)} copy(f32[3,4,8,128]{3,2,1,0:T(8,128)} %get-tuple-element.6) | data formatting | bytes 98304
  55.7 0.0 copy-done
  55.7 0.0 copy-start.1
  55.7 0.6 %copy.13 = f32[3,4,8,128]{3,2,1,0:T(8,128)} copy(f32[3,4,8,128]{3,2,1,0:T(8,128)S(1)} %copy-done) | data formatting | bytes 98304
  56.4 0.1 copy-done.1
  56.5 0.6 %copy.14 = f32[4,8,128]{2,1,0:T(8,128)} copy(f32[4,8,128]{2,1,0:T(8,128)S(1)} %copy-done.1) | data formatting | bytes 32768
Async XLA Ops:
  54.3 1.4 %copy-start = (f32[3,4,8,128]{3,2,1,0:T(8,128)S(1)}, f32[3,4,8,128]{3,2,1,0:T(8,128)}, u32[]{:S(2)}) copy-start(f32[3,4,8,128]{3,2,1,0:T(8,128)} %get-tuple-element.7) | copy-start | bytes 147460
  55.7 0.7 %copy-start.1 = (f32[4,8,128]{2,1,0:T(8,128)S(1)}, f32[4,8,128]{2,1,0:T(8,128)}, u32[]{:S(2)}) copy-start(f32[4,8,128]{2,1,0:T(8,128)} %get-tuple-element.8) | copy-start | bytes 49156

commit v3 on v1

v3 whole, which is shorter than its diff:
```python
import math

import jax
import jax.numpy as jnp
from jax import lax
from jax.experimental import pallas as pl
from jax.experimental.pallas import tpu as pltpu
from jax.sharding import PartitionSpec as P

stiff_floor = 0.001
damping = 0.6
coarse_damping = 0.5

MESH = pl.DeviceIdType.MESH
AXES = ("gx", "gy", "gz")
GROUPS = (24, 4, 8)
EDGE = 1.0
FACE = 2.0 - math.sqrt(2.0)
CORNER = 2.0 - math.sqrt(3.0)

LAME = 0.3 / (1.3 * 0.4)
SHEAR = 0.5 / 1.3
NORMAL = (LAME + 2.0 * SHEAR) / 16.0
CROSS = LAME / 16.0
TWIST = SHEAR / 16.0
BEND = (LAME + 2.0 * SHEAR + SHEAR) / 48.0
BEND_CROSS = LAME / 48.0
SPIN = SHEAR / 48.0
HOUR = (LAME + 2.0 * SHEAR + 2.0 * SHEAR) / 144.0
NODE_DIAG = (LAME + 2.0 * SHEAR + 2.0 * SHEAR) / 9.0

BOX = [(i, j, k) for i in (-1, 0, 1) for j in (-1, 0, 1) for k in (-1, 0, 1)]
BOX = sorted((b for b in BOX if any(b)), key=lambda b: (-sum(map(abs, b)), b[0] == 0))


def device(dx, dy, dz):
    return tuple(
        lax.rem(lax.axis_index(axis) + (step + count), count)
        for axis, step, count in zip(AXES, (dx, dy, dz), GROUPS)
    )


def partner():
    place = lax.axis_index("gx")
    return (place + 1 - 2 * lax.rem(place, 2), lax.axis_index("gy"), lax.axis_index("gz"))


def zp(v):
    return pltpu.roll(v, v.shape[1] - 1, 1)


def zm(v):
    return pltpu.roll(v, 1, 1)


def yp(v):
    return pltpu.roll(v, v.shape[0] - 1, 0)


def ym(v):
    return pltpu.roll(v, 1, 0)


def forward(field):
    modes = {}
    for c in range(3):
        u = field[c]
        up = zp(u)
        for r, w in ((0, u + up), (1, up - u)):
            wp = yp(w)
            modes[c, 0, r] = w + wp
            modes[c, 1, r] = wp - w
    return modes


def across(low, high):
    modes = {}
    for (c, q, r), a in low.items():
        b = high[c, q, r]
        if (q, r) != (0, 0):
            modes[c, 0, q, r] = a + b
        modes[c, 1, q, r] = b - a
    return modes


def stress(u):
    f = {}
    total = (u[0, 1, 0, 0] + u[1, 0, 1, 0] + u[2, 0, 0, 1]) * CROSS
    for c, mode in ((0, (1, 0, 0)), (1, (0, 1, 0)), (2, (0, 0, 1))):
        f[(c,) + mode] = u[(c,) + mode] * (NORMAL - CROSS) + total
    for a, b in (
        ((0, 0, 0, 1), (2, 1, 0, 0)),
        ((0, 0, 1, 0), (1, 1, 0, 0)),
        ((1, 0, 0, 1), (2, 0, 1, 0)),
    ):
        f[a] = f[b] = (u[a] + u[b]) * TWIST
    total = u[0, 0, 1, 1] + u[1, 1, 0, 1] + u[2, 1, 1, 0]
    for a in ((0, 0, 1, 1), (1, 1, 0, 1), (2, 1, 1, 0)):
        f[a] = (u[a] + total) * SPIN
    for a, b in (
        ((0, 1, 0, 1), (1, 0, 1, 1)),
        ((0, 1, 1, 0), (2, 0, 1, 1)),
        ((1, 1, 1, 0), (2, 1, 0, 1)),
    ):
        f[a] = u[a] * BEND + u[b] * BEND_CROSS
        f[b] = u[b] * BEND + u[a] * BEND_CROSS
    for c in range(3):
        f[c, 1, 1, 1] = u[c, 1, 1, 1] * HOUR
    return f


def scaled(f, factor):
    out, seen = {}, {}
    for mode, value in f.items():
        if id(value) not in seen:
            seen[id(value)] = value * factor
        out[mode] = seen[id(value)]
    return out


def backward(modes):
    rows = []
    for c in range(3):
        lines = []
        for r in (0, 1):
            s, d = modes[c, 0, r], modes[c, 1, r]
            lines.append((s - d) + ym(s + d))
        rows.append((lines[0] - lines[1]) + zm(lines[0] + lines[1]))
    return rows


def operator(field, factor, free, span, known):
    result, carry, low = {}, None, None
    for p in span:
        held = [free[p] * u for u in field[p]]
        high = known[p] if p in known else forward(held)
        if low is not None:
            f = scaled(stress(across(low, high)), factor[p - 1])
            here, later = {}, {}
            for c, q, r in low:
                d = f[c, 1, q, r]
                if (q, r) == (0, 0):
                    here[c, q, r] = -d
                    later[c, q, r] = d
                else:
                    s = f[c, 0, q, r]
                    here[c, q, r] = s - d
                    later[c, q, r] = s + d
            if carry is not None:
                rows = backward({mode: carry[mode] + here[mode] for mode in here})
                result[p - 1] = [
                    free[p - 1] * rows[c] + (field[p - 1][c] - last[c]) for c in range(3)
                ]
            carry = later
        low, last = high, held
    return result


def smooth_plane(v):
    along_z = zp(v) + zm(v)
    along_y = yp(v) + ym(v)
    both = yp(along_z) + ym(along_z)
    sides = along_z + along_y
    return 2.0 * v + EDGE * sides + FACE * both, EDGE * v + FACE * sides + CORNER * both


def smooth(planes):
    parts = [smooth_plane(v) for v in planes]
    return [
        parts[p][0] + (parts[p - 1][1] + parts[p + 1][1]) for p in range(1, len(planes) - 1)
    ]


def block_sum(low, high, even_y, even_z):
    v = low + high
    v = v + jnp.where(even_z, zp(v), zm(v))
    return v + jnp.where(even_y, yp(v), ym(v))


def iota(shape, dim):
    return lax.broadcasted_iota(jnp.int32, shape, dim)


def pack(tiles):
    slot = iota((8, 128), 1) >> 3
    packs = []
    for first in range(0, len(tiles), 16):
        total = None
        for s, tile in enumerate(tiles[first : first + 16]):
            turned = pltpu.roll(tile, (4 + 8 * s) % 128, 1)
            total = turned if total is None else jnp.where(slot == s, turned, total)
        packs.append(total)
    return packs


def unpack(packed, s):
    return pltpu.roll(packed, (124 - 8 * (s % 16)) % 128, 1)


def kernel(
    design_hbm, passive_hbm, fixed_hbm, state_hbm, adjoint_hbm, resid_hbm,
    adjoint_out, resid_out, grad_out,
    design, passive, fixed, own_sa, in_sem,
    own0, z0, lx0, ly0, lz0, lc0,
    own1, z1, lx1, ly1, lz1, lc1,
    z2, lx2, ly2, lz2, lc2,
    own3, z3, lx3, ly3, lz3, lc3,
    ar_send, ar_land, send_sem, recv_sem, relay_sem,
):
    copies = []

    def send(src, dst, target):
        number = len(copies)
        copy = pltpu.make_async_remote_copy(
            src_ref=src,
            dst_ref=dst,
            send_sem=send_sem.at[number],
            recv_sem=recv_sem.at[number],
            device_id=target,
            device_id_type=MESH,
        )
        copy.start()
        copies.append(copy)
        return copy

    def arrive(group):
        for copy in group:
            copy.wait_recv()

    def greet(semaphore, friends):
        for friend in friends:
            pl.semaphore_signal(semaphore, inc=1, device_id=device(*friend), device_id_type=MESH)

    barrier = pltpu.get_barrier_semaphore()
    greet(barrier, BOX)

    pairs = [(design_hbm, design), (passive_hbm, passive), (fixed_hbm, fixed)]
    for p, first in ((0, 0), (1, 3), (2, 14), (3, 17)):
        pairs.append((resid_hbm.at[:, p], own0.at[pl.ds(first, 3)]))
    pairs += [(adjoint_hbm, own_sa.at[pl.ds(0, 3)]), (state_hbm, own_sa.at[pl.ds(3, 3)])]
    inputs = [pltpu.make_async_copy(src, dst, in_sem.at[n]) for n, (src, dst) in enumerate(pairs)]
    for copy in inputs:
        copy.start()

    place_x, place_y, place_z = (lax.axis_index(axis) for axis in AXES)
    wide = (16, 256)
    row, lane = iota(wide, 0), iota(wide, 1)
    at_y = place_y * 8 + jnp.where(row < 12, row, row - 16)
    at_z = place_z * 128 + jnp.where(lane < 192, lane, lane - 256)
    inside = ((at_y >= 0) & (at_y < 32) & (at_z >= 0) & (at_z < 1024)).astype(jnp.float32)
    inside_low = inside * (place_x > 0).astype(jnp.float32)
    inside_high = inside * (place_x < 23).astype(jnp.float32)

    def sides(dim_at, count):
        return (dim_at > 0).astype(jnp.float32) + (dim_at < count - 1).astype(jnp.float32)

    near_y, near_z = sides(at_y, 32), sides(at_z, 1024)
    near, nearer = near_y + near_z, near_y * near_z
    weight_base = 2.0 + EDGE * near + FACE * nearer
    weight_step = EDGE + FACE * near + CORNER * nearer
    inverse_inner = 1.0 / (weight_base + 2.0 * weight_step)
    inverse_end = 1.0 / (weight_base + weight_step)
    inverse_first = jnp.where(place_x > 0, inverse_inner, inverse_end)
    inverse_last = jnp.where(place_x < 23, inverse_inner, inverse_end)

    def inverse_weight(p):
        return inverse_first if p == 0 else inverse_last if p == 3 else inverse_inner

    even_y, even_z = (row & 1) == 0, (lane & 1) == 0
    tile_even_y, tile_even_z = (iota((8, 128), 0) & 1) == 0, (iota((8, 128), 1) & 1) == 0
    top_half = iota((8, 128), 0) < 4
    low_slot = (iota((8, 128), 1) & 7) < 4

    free_at, masked_at = (6, 7, 8, 13), (9, 10, 11, 12)

    def resid_at(c, p):
        return 3 * p + c + (8 if p > 1 else 0)

    for copy in inputs[:3]:
        copy.wait()
    for p in range(4):
        code = passive[p]
        own0[masked_at[p]] = jnp.where(code == 1, 0.0, jnp.where(code == 2, 1.0, design[p]))
        own0[free_at[p]] = (1 - fixed[p]).astype(jnp.float32)
    for copy in inputs[3:7]:
        copy.wait()
    for n, packed in enumerate(pack([own0[t] for t in range(20)])):
        z0[n] = packed
    pl.semaphore_wait(barrier, len(BOX))

    def exchange(own, edges, land, tiles, packs):
        land_x, land_y, land_z, land_c = land
        near, far = [], []
        for i, j, k in BOX:
            target, slot = device(i, j, k), i + 1
            if k == 0:
                span = pl.ds(*tiles[slot])
                if j == 0:
                    copy = send(own.at[span], land_x.at[slot // 2, span], target)
                else:
                    half = pl.ds(2 * (j + 1), 4)
                    copy = send(own.at[span, half], land_y.at[slot, span, half], target)
            else:
                span = pl.ds(*packs[slot])
                if j == 0:
                    copy = send(edges.at[span], land_z.at[slot, (k + 1) // 2, span], target)
                else:
                    corner = j + 1 + (k + 1) // 2
                    copy = send(edges.at[span], land_c.at[slot, corner, span], target)
            (near if i == 0 else far).append(copy)
        return near, far

    def main_of(own, land, slot, t):
        tile = own[t] if slot == 1 else land[0][slot // 2, t]
        return jnp.concatenate([tile, land[1][slot, t]], 0)

    def edges_of(land, slot, n):
        land_z, land_c = land[2], land[3]
        top = jnp.where(low_slot, land_z[slot, 1, n], land_z[slot, 0, n])
        from_low_y = jnp.where(low_slot, land_c[slot, 3, n], land_c[slot, 2, n])
        from_high_y = jnp.where(low_slot, land_c[slot, 1, n], land_c[slot, 0, n])
        return jnp.concatenate([top, jnp.where(top_half, from_high_y, from_low_y)], 0)

    def widened(main, packed, s):
        return jnp.concatenate([main, unpack(packed, s)], 1)

    masks = (inside_high, inside, inside_low)

    land0 = (lx0, ly0, lz0, lc0)
    near, far = exchange(own0, z0, land0, ((0, 12), (0, 20), (7, 13)), ((0, 1), (0, 2), (0, 2)))
    arrive(near)
    edges0 = {(1, n): edges_of(land0, 1, n) for n in range(2)}

    def input_plane(slot, t):
        return widened(main_of(own0, land0, slot, t), edges0[slot, t // 16], t) * masks[slot]

    masked = {p: input_plane(1, masked_at[p]) for p in range(4)}
    parts = {p: smooth_plane(masked[p]) for p in range(4)}
    free = {p: input_plane(1, free_at[p]) for p in range(4)}
    resid = {p: [input_plane(1, resid_at(c, p)) for c in range(3)] for p in range(4)}
    arrive(far)
    edges0[0, 0] = edges_of(land0, 0, 0)
    for n in range(2):
        edges0[2, n] = edges_of(land0, 2, n)
    for p in range(3):
        parts[p + 4] = smooth_plane(input_plane(0, masked_at[p]))
        free[p + 4] = input_plane(0, free_at[p])
    for p in range(4):
        parts[p - 4] = smooth_plane(input_plane(2, masked_at[p]))
    for p in range(1, 4):
        free[p - 4] = input_plane(2, free_at[p])
    for p in range(2):
        resid[p + 4] = [input_plane(0, resid_at(c, p)) for c in range(3)]
        resid[p - 2] = [input_plane(2, resid_at(c, p + 2)) for c in range(3)]
    greet(relay_sem.at[0], [(2, 0, 0), (-2, 0, 0)])
    greet(relay_sem.at[1], [(0, 0, 2), (0, 0, -2)])

    density, factor, paired = {}, {}, {}
    for p in range(-3, 6):
        d = (parts[p][0] + (parts[p - 1][1] + parts[p + 1][1])) * inverse_weight(p)
        density[p] = d
        f = stiff_floor + d * d * d * (1.0 - stiff_floor)
        factor[p] = f * (inside_low if p < 0 else inside if p < 4 else inside_high)
        v = factor[p] + zm(factor[p])
        paired[p] = v + ym(v)

    diagonal, inverse_diag, first = {}, {}, {}
    for p in range(-2, 6):
        diagonal[p] = free[p] * (NODE_DIAG * (paired[p] + paired[p - 1])) + (1.0 - free[p])
        inverse_diag[p] = 1.0 / diagonal[p]
        first[p] = [damping * resid[p][c] * inverse_diag[p] for c in range(3)]

    def apply(field, lowest, highest, known=None):
        span = range(lowest - 1, highest + 2)
        return operator(field, factor, free, span, known or {})

    image = apply(first, 0, 3)
    second = [
        [(resid[p][c] - image[p][c])[0:8, 0:128] for c in range(3)] for p in range(4)
    ]
    inverse_coarse = {}
    for k in range(2):
        total = block_sum(diagonal[2 * k], diagonal[2 * k + 1], even_y, even_z)
        inverse_coarse[k] = 1.0 / total
    coarse_own = []
    for k in range(2):
        for c in range(3):
            total = block_sum(second[2 * k][c], second[2 * k + 1][c], tile_even_y, tile_even_z)
            coarse_own.append(coarse_damping * total * inverse_coarse[k][0:8, 0:128])
    for t in range(6):
        own1[t] = coarse_own[t]
    z1[0] = pack(coarse_own)[0]
    land1 = (lx1, ly1, lz1, lc1)
    near, far = exchange(own1, z1, land1, ((0, 6),) * 3, ((0, 1),) * 3)

    for copy in inputs[7:]:
        copy.wait()
    for n, packed in enumerate(pack([own_sa[f, p] for p in range(4) for f in range(6)])):
        z2[n] = packed
    top_row = pl.ds(0, 1)
    group2 = [
        send(z2.at[pl.ds(0, 1)], lc2.at[1, pl.ds(0, 1)], device(-1, -1, -1)),
        send(z2, lc2.at[0], device(0, -1, -1)),
        send(z2.at[pl.ds(0, 1)], lz2.at[1, pl.ds(0, 1)], device(-1, 0, -1)),
        send(own_sa.at[:, 0, top_row], ly2.at[:, 4, top_row], device(-1, -1, 0)),
        send(own_sa.at[:, 0], lx2, device(-1, 0, 0)),
        send(own_sa.at[:, :, top_row], ly2.at[:, pl.ds(0, 4), top_row], device(0, -1, 0)),
        send(z2, lz2.at[0], device(0, 0, -1)),
    ]
    pl.semaphore_wait(relay_sem.at[0], 2)
    greet(relay_sem.at[2], [(4, 0, 0), (-4, 0, 0)])
    for k in (-1, 2):
        total = block_sum(diagonal[2 * k], diagonal[2 * k + 1], even_y, even_z)
        inverse_coarse[k] = 1.0 / total

    arrive(near)
    coarse = {}

    def coarse_plane(slot, k):
        edges = edges_of(land1, slot, 0)
        return [
            widened(main_of(own1, land1, slot, 3 * k + c), edges, 3 * k + c) * masks[slot]
            for c in range(3)
        ]

    for k in range(2):
        coarse[k] = coarse_plane(1, k)
    known = {p: forward([free[p] * u for u in coarse[p // 2]]) for p in range(4)}
    arrive(far)
    for k in range(2):
        coarse[k - 2] = coarse_plane(2, k)
        coarse[k + 2] = coarse_plane(0, k)
    pl.semaphore_wait(relay_sem.at[1], 2)
    pl.semaphore_wait(relay_sem.at[2], 2)
    greet(relay_sem.at[3], [(8, 0, 0), (-8, 0, 0)])
    spread = {p: coarse[p // 2] for p in range(-4, 8)}
    image = apply(spread, -2, 5, known)
    middle = {}
    for k in range(-1, 3):
        for c in range(3):
            total = block_sum(image[2 * k][c], image[2 * k + 1][c], even_y, even_z)
            fix = 2.0 * coarse[k][c] - coarse_damping * total * inverse_coarse[k]
            for p in (2 * k, 2 * k + 1):
                middle.setdefault(p, []).append(first[p][c] + fix)
    image = apply(middle, -1, 4)
    direction = {
        p: [
            middle[p][c] + damping * (resid[p][c] - image[p][c]) * inverse_diag[p]
            for c in range(3)
        ]
        for p in range(-1, 5)
    }
    image = apply(direction, 0, 3)
    image = {p: [image[p][c][0:8, 0:128] for c in range(3)] for p in range(4)}
    numerator = denominator = None
    for p in range(4):
        for c in range(3):
            d = direction[p][c][0:8, 0:128]
            a, b = resid[p][c][0:8, 0:128] * d, d * image[p][c]
            numerator = a if numerator is None else numerator + a
            denominator = b if denominator is None else denominator + b
    numerator = numerator + pltpu.roll(numerator, 4, 0)
    denominator = denominator + pltpu.roll(denominator, 4, 0)
    sums = jnp.where(top_half, numerator, denominator)

    landed = [0]

    def spread_sums(stage, value, targets):
        ar_send[stage] = value
        base = landed[0]
        landed[0] += len(targets)
        group = [
            send(ar_send.at[stage], ar_land.at[base + n], target)
            for n, target in enumerate(targets)
        ]

        def gather():
            arrive(group)
            total = value
            for n in range(len(targets)):
                total = total + ar_land[base + n]
            return total

        return gather

    sums = spread_sums(0, sums, [partner()])()
    pl.semaphore_wait(relay_sem.at[3], 2)
    gather = spread_sums(1, sums, [device(2 * i, 0, 0) for i in (6, 5, 7, 4, 8, 3, 9, 2, 10, 1, 11)])
    arrive(group2)

    edges2 = [jnp.concatenate([lz2[0, n], lc2[0, n]], 0) for n in range(2)]
    edges2_high = jnp.concatenate([lz2[1, 0], lc2[1, 0]], 0)

    def ends(f, p):
        if p < 4:
            main = jnp.concatenate([own_sa[f, p], ly2[f, p]], 0)
            return widened(main, edges2[(6 * p + f) // 16], 6 * p + f) * inside
        main = jnp.concatenate([lx2[f], ly2[f, 4]], 0)
        return widened(main, edges2_high, f) * inside_high

    def corner_modes(fields):
        return [{m: v[0:8, 0:128] for m, v in forward(fields[p]).items()} for p in range(5)]

    adjoint_modes = corner_modes([[ends(c, p) for c in range(3)] for p in range(5)])
    state_modes = corner_modes([[ends(3 + c, p) for c in range(3)] for p in range(5)])
    direction_modes = corner_modes([direction[p] for p in range(5)])
    sens = []
    for p in range(4):
        force = stress(across(state_modes[p], state_modes[p + 1]))
        d = density[p][0:8, 0:128]
        weight = 3.0 * (1.0 - stiff_floor) * d * d * inverse_weight(p)[0:8, 0:128]
        for modes in (adjoint_modes, direction_modes):
            with_modes = across(modes[p], modes[p + 1])
            energy = None
            for mode, value in force.items():
                term = with_modes[mode] * value
                energy = term if energy is None else energy + term
            sens.append(weight * energy)
    for t in range(8):
        own3[t] = sens[t]
    z3[0] = pack(sens)[0]
    land3 = (lx3, ly3, lz3, lc3)
    near, far = exchange(own3, z3, land3, ((0, 2), (0, 8), (6, 2)), ((0, 1),) * 3)
    sums = gather()
    gather = spread_sums(2, sums, [device(0, 0, k) for k in (4, 3, 5, 2, 6, 1, 7)])
    arrive(near)
    arrive(far)
    edges3 = [edges_of(land3, slot, 0) for slot in range(3)]

    def sens_plane(slot, t):
        return widened(main_of(own3, land3, slot, t), edges3[slot], t) * masks[slot]

    grads = []
    for f in range(2):
        planes = [sens_plane(2, 6 + f)]
        planes += [sens_plane(1, 2 * p + f) for p in range(4)]
        planes += [sens_plane(0, f)]
        grads.append([v[0:8, 0:128] for v in smooth(planes)])
    sums = gather()
    sums = spread_sums(3, sums, [device(0, j, 0) for j in (2, 1, 3)])()
    numerator = jnp.sum(jnp.where(top_half, sums, 0.0), axis=(0, 1), keepdims=True)
    denominator = jnp.sum(jnp.where(top_half, 0.0, sums), axis=(0, 1), keepdims=True)
    step = jnp.broadcast_to(numerator / denominator, (8, 128))
    for p in range(4):
        for c in range(3):
            adjoint_out[c, p] = own_sa[c, p] + step * direction[p][c][0:8, 0:128]
            resid_out[c, p] = own0[resid_at(c, p)] - step * image[p][c]
        grad_out[p] = jnp.where(passive[p] == 0, grads[0][p] + step * grads[1][p], 0.0)
    for copy in copies:
        copy.wait_send()


def body(design, passive, fixed, state, adjoint, resid):
    def scratch(*shape):
        return pltpu.VMEM(shape, jnp.float32)

    def landing(tiles, packs):
        return [
            scratch(2, tiles, 8, 128),
            scratch(3, tiles, 8, 128),
            scratch(3, 2, packs, 8, 128),
            scratch(3, 4, packs, 8, 128),
        ]

    n_copies = 3 * 26 + 7 + 22
    return pl.pallas_call(
        kernel,
        out_shape=(
            pltpu.VMEM((3, 4, 8, 128), jnp.float32),
            pltpu.VMEM((3, 4, 8, 128), jnp.float32),
            pltpu.VMEM((4, 8, 128), jnp.float32),
        ),
        in_specs=[pl.BlockSpec(memory_space=pl.ANY)] * 6,
        out_specs=(pl.BlockSpec(memory_space=pltpu.VMEM),) * 3,
        scratch_shapes=[
            scratch(4, 8, 128),
            pltpu.VMEM((4, 8, 128), jnp.int32),
            pltpu.VMEM((4, 8, 128), jnp.int32),
            scratch(6, 4, 8, 128),
            pltpu.SemaphoreType.DMA((9,)),
            scratch(20, 8, 128),
            scratch(2, 8, 128),
            *landing(20, 2),
            scratch(6, 8, 128),
            scratch(1, 8, 128),
            *landing(6, 1),
            scratch(2, 8, 128),
            scratch(6, 8, 128),
            scratch(6, 5, 8, 128),
            scratch(2, 2, 8, 128),
            scratch(2, 2, 8, 128),
            scratch(8, 8, 128),
            scratch(1, 8, 128),
            *landing(8, 1),
            scratch(4, 8, 128),
            scratch(22, 8, 128),
            pltpu.SemaphoreType.DMA((n_copies,)),
            pltpu.SemaphoreType.DMA((n_copies,)),
            pltpu.SemaphoreType.REGULAR((4,)),
        ],
        compiler_params=pltpu.CompilerParams(
            collective_id=0, has_side_effects=True, vmem_limit_bytes=62 * 2**20
        ),
    )(design, passive, fixed, state, adjoint, resid)


def solution(mesh):
    return jax.shard_map(
        body,
        mesh=mesh,
        in_specs=(P("gx", "gy", "gz"),) * 3 + (P(None, "gx", "gy", "gz"),) * 3,
        out_specs=(P(None, "gx", "gy", "gz"), P(None, "gx", "gy", "gz"), P("gx", "gy", "gz")),
        check_vma=False,
    )
```

time: 61.1 us -> 51.1 us (0.84)
  the two profiles are of different devices: /device:TPU:1 before, /device:TPU:2 now
where the time goes in v3:
time: 51.1 us; the launch traced here: 50.9 us
  Pallas kernels  48.4 us (95%)
  local copies, waits for them, and re-layouts  1.85 us (4%)
  between operations  0.64 us (1%)
    pallas_call x1, Pallas kernels, body(): pl.pallas_call(kernel, out_shape=(pltpu.VMEM((3, 4, 8, 128), jnp.float32)...  48.4 us
    unnamed x3, local copies, waits for them, and re-layouts  1.85 us

profile of v3, /device:TPU:2, one launch (start us, length us, event | category | flops | bytes accessed | tf_op | source)
XLA Modules:
  0.0 50.9 jit_solution(8607686063673048495)
XLA Ops:
  0.6 48.4 %shard_map.85 = (f32[3,4,8,128]{3,2,1,0:T(8,128)S(1)}, f32[3,4,8,128]{3,2,1,0:T(8,128)S(1)}, f32[4,8,128]{2,1,0:T(8,128)S(1)}) custom-call(f32[4,8,128]{2,1,0:T(8,128)} %design_hbm.1, s32[4,8,128]{2,1,0:T(8,128)} %passive_hbm.1, s32[4,8,128]{2,1,0:T(8,128)} %fixed_hbm.1, f32[3,4,8,128]{3,2,1,0:T(8,128)} %state_hbm.1, f32[3,4,8,128]{3,2,1,0:T(8,128)} %adjoint_hbm.1, ...), custom_call_target="tpu_custom_call" | custom-call | tf_op jit(solution)/shard_map/pallas_call | solution.py:566
  49.0 0.6 %copy.12 = f32[3,4,8,128]{3,2,1,0:T(8,128)} copy(f32[3,4,8,128]{3,2,1,0:T(8,128)S(1)} %get-tuple-element.3) | data formatting | bytes 98304
  49.6 0.6 %copy.14 = f32[4,8,128]{2,1,0:T(8,128)} copy(f32[4,8,128]{2,1,0:T(8,128)S(1)} %get-tuple-element.5) | data formatting | bytes 32768
  50.2 0.6 %copy.13 = f32[3,4,8,128]{3,2,1,0:T(8,128)} copy(f32[3,4,8,128]{3,2,1,0:T(8,128)S(1)} %get-tuple-element.4) | data formatting | bytes 98304

commit v4 on v3

--- a/solution.py
+++ b/solution.py
@@ -129,13 +129,16 @@
     return rows
 
 
-def operator(field, factor, free, span, known):
+def operator(field, factor, free, span, known, ready):
     result, carry, low = {}, None, None
     for p in span:
         held = [free[p] * u for u in field[p]]
         high = known[p] if p in known else forward(held)
         if low is not None:
-            f = scaled(stress(across(low, high)), factor[p - 1])
+            if p - 1 in ready:
+                f = ready[p - 1]
+            else:
+                f = scaled(stress(across(low, high)), factor[p - 1])
             here, later = {}, {}
             for c, q, r in low:
                 d = f[c, 1, q, r]
@@ -199,7 +202,7 @@
 
 def kernel(
     design_hbm, passive_hbm, fixed_hbm, state_hbm, adjoint_hbm, resid_hbm,
-    adjoint_out, resid_out, grad_out,
+    direction_out, image_out, grads_out, step_out,
     design, passive, fixed, own_sa, in_sem,
     own0, z0, lx0, ly0, lz0, lc0,
     own1, z1, lx1, ly1, lz1, lc1,
@@ -207,7 +210,12 @@
     own3, z3, lx3, ly3, lz3, lc3,
     ar_send, ar_land, send_sem, recv_sem, relay_sem,
 ):
-    copies = []
+    copies, sent = [], [0]
+
+    def settle():
+        for copy in copies[sent[0] :]:
+            copy.wait_send()
+        sent[0] = len(copies)
 
     def send(src, dst, target):
         number = len(copies)
@@ -231,9 +239,6 @@
         for friend in friends:
             pl.semaphore_signal(semaphore, inc=1, device_id=device(*friend), device_id_type=MESH)
 
-    barrier = pltpu.get_barrier_semaphore()
-    greet(barrier, BOX)
-
     pairs = [(design_hbm, design), (passive_hbm, passive), (fixed_hbm, fixed)]
     for p, first in ((0, 0), (1, 3), (2, 14), (3, 17)):
         pairs.append((resid_hbm.at[:, p], own0.at[pl.ds(first, 3)]))
@@ -241,6 +246,10 @@
     inputs = [pltpu.make_async_copy(src, dst, in_sem.at[n]) for n, (src, dst) in enumerate(pairs)]
     for copy in inputs:
         copy.start()
+
+    barrier = pltpu.get_barrier_semaphore()
+    greeted = BOX + [(2, 0, 0), (-2, 0, 0)]
+    greet(barrier, greeted)
 
     place_x, place_y, place_z = (lax.axis_index(axis) for axis in AXES)
     wide = (16, 256)
@@ -286,7 +295,7 @@
         copy.wait()
     for n, packed in enumerate(pack([own0[t] for t in range(20)])):
         z0[n] = packed
-    pl.semaphore_wait(barrier, len(BOX))
+    pl.semaphore_wait(barrier, len(greeted))
 
     def exchange(own, edges, land, tiles, packs):
         land_x, land_y, land_z, land_c = land
@@ -328,6 +337,7 @@
 
     land0 = (lx0, ly0, lz0, lc0)
     near, far = exchange(own0, z0, land0, ((0, 12), (0, 20), (7, 13)), ((0, 1), (0, 2), (0, 2)))
+    greet(relay_sem.at[0], [(2, 0, 0), (-2, 0, 0)])
     arrive(near)
     edges0 = {(1, n): edges_of(land0, 1, n) for n in range(2)}
 
@@ -338,25 +348,30 @@
     parts = {p: smooth_plane(masked[p]) for p in range(4)}
     free = {p: input_plane(1, free_at[p]) for p in range(4)}
     resid = {p: [input_plane(1, resid_at(c, p)) for c in range(3)] for p in range(4)}
+    density, factor, paired = {}, {}, {}
+    diagonal, inverse_diag, first = {}, {}, {}
     arrive(far)
     edges0[0, 0] = edges_of(land0, 0, 0)
     for n in range(2):
         edges0[2, n] = edges_of(land0, 2, n)
-    for p in range(3):
-        parts[p + 4] = smooth_plane(input_plane(0, masked_at[p]))
-        free[p + 4] = input_plane(0, free_at[p])
-    for p in range(4):
-        parts[p - 4] = smooth_plane(input_plane(2, masked_at[p]))
-    for p in range(1, 4):
-        free[p - 4] = input_plane(2, free_at[p])
-    for p in range(2):
-        resid[p + 4] = [input_plane(0, resid_at(c, p)) for c in range(3)]
-        resid[p - 2] = [input_plane(2, resid_at(c, p + 2)) for c in range(3)]
-    greet(relay_sem.at[0], [(2, 0, 0), (-2, 0, 0)])
     greet(relay_sem.at[1], [(0, 0, 2), (0, 0, -2)])
-
-    density, factor, paired = {}, {}, {}
-    for p in range(-3, 6):
+    pl.semaphore_wait(relay_sem.at[0], 2)
+    greet(relay_sem.at[2], [(4, 0, 0), (-4, 0, 0)])
+
+    def beyond(p):
+        return (2, p + 4) if p < 0 else (0, p - 4)
+
+    def take_masked(p):
+        slot, q = beyond(p)
+        parts[p] = smooth_plane(input_plane(slot, masked_at[q]))
+
+    def take_nodes(p):
+        slot, q = beyond(p)
+        free[p] = input_plane(slot, free_at[q])
+        if -3 < p < 6:
+            resid[p] = [input_plane(slot, resid_at(c, q)) for c in range(3)]
+
+    def take_element(p):
         d = (parts[p][0] + (parts[p - 1][1] + parts[p + 1][1])) * inverse_weight(p)
         density[p] = d
         f = stiff_floor + d * d * d * (1.0 - stiff_floor)
@@ -364,15 +379,24 @@
         v = factor[p] + zm(factor[p])
         paired[p] = v + ym(v)
 
-    diagonal, inverse_diag, first = {}, {}, {}
-    for p in range(-2, 6):
+    def take_diagonal(p):
         diagonal[p] = free[p] * (NODE_DIAG * (paired[p] + paired[p - 1])) + (1.0 - free[p])
         inverse_diag[p] = 1.0 / diagonal[p]
         first[p] = [damping * resid[p][c] * inverse_diag[p] for c in range(3)]
 
-    def apply(field, lowest, highest, known=None):
+    for p in (-3, -2, -1, 4, 5):
+        take_masked(p)
+    for p in (-1, 4):
+        take_nodes(p)
+    for p in range(-2, 5):
+        if p not in density:
+            take_element(p)
+    for p in range(-1, 5):
+        take_diagonal(p)
+
+    def apply(field, lowest, highest, known=None, ready=None):
         span = range(lowest - 1, highest + 2)
-        return operator(field, factor, free, span, known or {})
+        return operator(field, factor, free, span, known or {}, ready or {})
 
     image = apply(first, 0, 3)
     second = [
@@ -407,8 +431,16 @@
         send(own_sa.at[:, :, top_row], ly2.at[:, pl.ds(0, 4), top_row], device(0, -1, 0)),
         send(z2, lz2.at[0], device(0, 0, -1)),
     ]
-    pl.semaphore_wait(relay_sem.at[0], 2)
-    greet(relay_sem.at[2], [(4, 0, 0), (-4, 0, 0)])
+    pl.semaphore_wait(relay_sem.at[2], 2)
+    greet(relay_sem.at[3], [(8, 0, 0), (-8, 0, 0)])
+    for p in (-4, 6):
+        take_masked(p)
+    for p in (-3, -2, 5, 6):
+        take_nodes(p)
+    for p in (-3, 5):
+        take_element(p)
+    for p in (-2, 5):
+        take_diagonal(p)
     for k in (-1, 2):
         total = block_sum(diagonal[2 * k], diagonal[2 * k + 1], even_y, even_z)
         inverse_coarse[k] = 1.0 / total
@@ -426,15 +458,14 @@
     for k in range(2):
         coarse[k] = coarse_plane(1, k)
     known = {p: forward([free[p] * u for u in coarse[p // 2]]) for p in range(4)}
+    ready = {p: scaled(stress(across(known[p], known[p + 1])), factor[p]) for p in range(3)}
     arrive(far)
     for k in range(2):
         coarse[k - 2] = coarse_plane(2, k)
         coarse[k + 2] = coarse_plane(0, k)
     pl.semaphore_wait(relay_sem.at[1], 2)
-    pl.semaphore_wait(relay_sem.at[2], 2)
-    greet(relay_sem.at[3], [(8, 0, 0), (-8, 0, 0)])
     spread = {p: coarse[p // 2] for p in range(-4, 8)}
-    image = apply(spread, -2, 5, known)
+    image = apply(spread, -2, 5, known, ready)
     middle = {}
     for k in range(-1, 3):
         for c in range(3):
@@ -442,23 +473,35 @@
             fix = 2.0 * coarse[k][c] - coarse_damping * total * inverse_coarse[k]
             for p in (2 * k, 2 * k + 1):
                 middle.setdefault(p, []).append(first[p][c] + fix)
-    image = apply(middle, -1, 4)
-    direction = {
-        p: [
-            middle[p][c] + damping * (resid[p][c] - image[p][c]) * inverse_diag[p]
-            for c in range(3)
-        ]
-        for p in range(-1, 5)
-    }
-    image = apply(direction, 0, 3)
-    image = {p: [image[p][c][0:8, 0:128] for c in range(3)] for p in range(4)}
+    direction = {}
+
+    def smoothed_again(lowest, highest):
+        image = apply(middle, lowest, highest)
+        for p in range(lowest, highest + 1):
+            direction[p] = [
+                middle[p][c] + damping * (resid[p][c] - image[p][c]) * inverse_diag[p]
+                for c in range(3)
+            ]
+
+    smoothed_again(0, 4)
+    held_modes = {p: forward([free[p] * d for d in direction[p]]) for p in range(5)}
     numerator = denominator = None
     for p in range(4):
+        u = across(*({m: v[0:8, 0:128] for m, v in held_modes[p + n].items()} for n in range(2)))
+        energy = None
+        for mode, value in stress(u).items():
+            term = u[mode] * value
+            energy = term if energy is None else energy + term
+        b = factor[p][0:8, 0:128] * energy
+        fixed_part = None
         for c in range(3):
             d = direction[p][c][0:8, 0:128]
-            a, b = resid[p][c][0:8, 0:128] * d, d * image[p][c]
+            direction_out[c, p] = d
+            a = resid[p][c][0:8, 0:128] * d
             numerator = a if numerator is None else numerator + a
-            denominator = b if denominator is None else denominator + b
+            fixed_part = d * d if fixed_part is None else fixed_part + d * d
+        b = b + (1.0 - free[p][0:8, 0:128]) * fixed_part
+        denominator = b if denominator is None else denominator + b
     numerator = numerator + pltpu.roll(numerator, 4, 0)
     denominator = denominator + pltpu.roll(denominator, 4, 0)
     sums = jnp.where(top_half, numerator, denominator)
@@ -484,8 +527,7 @@
         return gather
 
     sums = spread_sums(0, sums, [partner()])()
-    pl.semaphore_wait(relay_sem.at[3], 2)
-    gather = spread_sums(1, sums, [device(2 * i, 0, 0) for i in (6, 5, 7, 4, 8, 3, 9, 2, 10, 1, 11)])
+    gather = spread_sums(1, sums, [device(0, 0, k) for k in (4, 3, 5, 2, 6, 1, 7)])
     arrive(group2)
 
     edges2 = [jnp.concatenate([lz2[0, n], lc2[0, n]], 0) for n in range(2)]
@@ -520,9 +562,17 @@
         own3[t] = sens[t]
     z3[0] = pack(sens)[0]
     land3 = (lx3, ly3, lz3, lc3)
+    settle()
     near, far = exchange(own3, z3, land3, ((0, 2), (0, 8), (6, 2)), ((0, 1),) * 3)
+    smoothed_again(-1, -1)
+    image = apply(direction, 0, 3, held_modes)
+    for p in range(4):
+        for c in range(3):
+            image_out[c, p] = image[p][c][0:8, 0:128]
     sums = gather()
-    gather = spread_sums(2, sums, [device(0, 0, k) for k in (4, 3, 5, 2, 6, 1, 7)])
+    sums = spread_sums(2, sums, [device(0, j, 0) for j in (2, 1, 3)])()
+    pl.semaphore_wait(relay_sem.at[3], 2)
+    gather = spread_sums(3, sums, [device(2 * i, 0, 0) for i in (6, 5, 7, 4, 8, 3, 9, 2, 10, 1, 11)])
     arrive(near)
     arrive(far)
     edges3 = [edges_of(land3, slot, 0) for slot in range(3)]
@@ -530,24 +580,18 @@
     def sens_plane(slot, t):
         return widened(main_of(own3, land3, slot, t), edges3[slot], t) * masks[slot]
 
-    grads = []
     for f in range(2):
         planes = [sens_plane(2, 6 + f)]
         planes += [sens_plane(1, 2 * p + f) for p in range(4)]
         planes += [sens_plane(0, f)]
-        grads.append([v[0:8, 0:128] for v in smooth(planes)])
+        for p, v in enumerate(smooth(planes)):
+            grads_out[f, p] = v[0:8, 0:128]
+    settle()
     sums = gather()
-    sums = spread_sums(3, sums, [device(0, j, 0) for j in (2, 1, 3)])()
     numerator = jnp.sum(jnp.where(top_half, sums, 0.0), axis=(0, 1), keepdims=True)
     denominator = jnp.sum(jnp.where(top_half, 0.0, sums), axis=(0, 1), keepdims=True)
-    step = jnp.broadcast_to(numerator / denominator, (8, 128))
-    for p in range(4):
-        for c in range(3):
-            adjoint_out[c, p] = own_sa[c, p] + step * direction[p][c][0:8, 0:128]
-            resid_out[c, p] = own0[resid_at(c, p)] - step * image[p][c]
-        grad_out[p] = jnp.where(passive[p] == 0, grads[0][p] + step * grads[1][p], 0.0)
-    for copy in copies:
-        copy.wait_send()
+    step_out[...] = jnp.broadcast_to(numerator / denominator, (8, 128))
+    settle()
 
 
 def body(design, passive, fixed, state, adjoint, resid):
@@ -563,15 +607,16 @@
         ]
 
     n_copies = 3 * 26 + 7 + 22
-    return pl.pallas_call(
+    direction, image, grads, step = pl.pallas_call(
         kernel,
         out_shape=(
             pltpu.VMEM((3, 4, 8, 128), jnp.float32),
             pltpu.VMEM((3, 4, 8, 128), jnp.float32),
-            pltpu.VMEM((4, 8, 128), jnp.float32),
+            pltpu.VMEM((2, 4, 8, 128), jnp.float32),
+            pltpu.VMEM((8, 128), jnp.float32),
         ),
         in_specs=[pl.BlockSpec(memory_space=pl.ANY)] * 6,
-        out_specs=(pl.BlockSpec(memory_space=pltpu.VMEM),) * 3,
+        out_specs=(pl.BlockSpec(memory_space=pltpu.VMEM),) * 4,
         scratch_shapes=[
             scratch(4, 8, 128),
             pltpu.VMEM((4, 8, 128), jnp.int32),
@@ -602,6 +647,11 @@
             collective_id=0, has_side_effects=True, vmem_limit_bytes=62 * 2**20
         ),
     )(design, passive, fixed, state, adjoint, resid)
+    return (
+        adjoint + step * direction,
+        resid - step * image,
+        jnp.where(passive == 0, grads[0] + step * grads[1], 0.0),
+    )
 
 
 def solution(mesh):

time: 51.1 us -> 49.6 us (0.971)
  local copies, waits for them, and re-layouts: 1.85 us -> 0.06 us
  other arithmetic: 0 us -> 1.27 us
  Pallas kernels: 48.4 us -> 47.2 us
    unnamed x3 -> x6, local copies, waits for them, and re-layouts: 1.85 us -> 0.06 us
    pallas_call x1, Pallas kernels: 48.4 us -> 47.2 us  [body(): pl.pallas_call(kernel, out_shape=(pltpu.VMEM((3, 4, 8, 128), jnp.float32)...]
    sub x0 -> x1, other arithmetic: none -> 0.66 us  [body(): resid - step * image]
    select_n x0 -> x1, other arithmetic: none -> 0.61 us  [body(): jnp.where(passive == 0, grads[0] + step * grads[1], 0.0)]
where the time goes in v4:
time: 49.6 us; the launch traced here: 49.3 us
  Pallas kernels  47.2 us (95%)
  other arithmetic  1.27 us (3%)
  between operations  0.68 us (1%)
    pallas_call x1, Pallas kernels, body(): pl.pallas_call(kernel, out_shape=(pltpu.VMEM((3, 4, 8, 128), jnp.float32)...  47.2 us

profile of v4, /device:TPU:2, one launch (start us, length us, event | category | flops | bytes accessed | tf_op | source)
XLA Modules:
  0.0 49.3 jit_solution(6718287405779564923)
XLA Ops:
  0.6 0.0 copy-start
  0.6 0.0 copy-start.1
  0.7 47.2 %shard_map.85 = (f32[3,4,8,128]{3,2,1,0:T(8,128)S(1)}, f32[3,4,8,128]{3,2,1,0:T(8,128)S(1)}, f32[2,4,8,128]{3,2,1,0:T(8,128)S(1)}, f32[8,128]{1,0:T(8,128)S(1)}) custom-call(f32[4,8,128]{2,1,0:T(8,128)} %design_hbm.1, s32[4,8,128]{2,1,0:T(8,128)} %passive_hbm.1, s32[4,8,128]{2,1,0:T(8,128)} %fixed_hbm.1, f32[3,4,8,128]{3,2,1,0:T(8,128)} %state_hbm.1, ...), custom_call_target="tpu_custom_call" | custom-call | tf_op jit(solution)/shard_map/pallas_call | solution.py:610
  47.9 0.0 copy-done
  47.9 0.0 copy-done.1
  47.9 0.0 copy-start.2
  47.9 0.7 %multiply_subtract_fusion = (f32[3,4,8,128]{3,2,1,0:T(8,128)}, f32[3,4,8,128]{3,2,1,0:T(8,128)}) fusion(f32[3,4,8,128]{3,2,1,0:T(8,128)S(1)} %copy-done, f32[3,4,8,128]{3,2,1,0:T(8,128)S(1)} %get-tuple-element.9, f32[8,128]{1,0:T(8,128)S(1)} %get-tuple-element.7, f32[3,4,8,128]{3,2,1,0:T(8,128)S(1)} %copy-done.1, f32[3,4,8,128]{3,2,1,0:T(8,128)S(1)} %get-tuple-element.8), kind=kLoop, calls=%fused_computation | loop fusion | flops 49152 | bytes 299008 | tf_op jit(solution)/shard_map/sub | solution.py:652
  48.6 0.0 copy-done.2
  48.6 0.6 %fusion.1 = f32[4,8,128]{2,1,0:T(8,128)} fusion(f32[2,4,8,128]{3,2,1,0:T(8,128)S(1)} %get-tuple-element.10, s32[4,8,128]{2,1,0:T(8,128)S(1)} %copy-done.2, f32[8,128]{1,0:T(8,128)S(1)} %get-tuple-element.7), kind=kLoop, calls=%fused_computation.4 | loop fusion | flops 16384 | bytes 69632 | tf_op jit(solution)/shard_map/jit(_where)/select_n | solution.py:653
Async XLA Ops:
  0.6 47.3 %copy-start = (f32[3,4,8,128]{3,2,1,0:T(8,128)S(1)}, f32[3,4,8,128]{3,2,1,0:T(8,128)}, u32[]{:S(2)}) copy-start(f32[3,4,8,128]{3,2,1,0:T(8,128)} %resid_hbm.1) | copy-start | bytes 147460
  0.6 47.3 %copy-start.1 = (f32[3,4,8,128]{3,2,1,0:T(8,128)S(1)}, f32[3,4,8,128]{3,2,1,0:T(8,128)}, u32[]{:S(2)}) copy-start(f32[3,4,8,128]{3,2,1,0:T(8,128)} %adjoint_hbm.1) | copy-start | bytes 147460
  47.9 0.7 %copy-start.2 = (s32[4,8,128]{2,1,0:T(8,128)S(1)}, s32[4,8,128]{2,1,0:T(8,128)}, u32[]{:S(2)}) copy-start(s32[4,8,128]{2,1,0:T(8,128)} %passive_hbm.1) | copy-start | bytes 49156

commit v5 on v4

--- a/solution.py
+++ b/solution.py
@@ -32,17 +32,16 @@
 BOX = [(i, j, k) for i in (-1, 0, 1) for j in (-1, 0, 1) for k in (-1, 0, 1)]
 BOX = sorted((b for b in BOX if any(b)), key=lambda b: (-sum(map(abs, b)), b[0] == 0))
 
+FLAT = [(j, k) for j in range(4) for k in range(8) if j or k]
+FLAT.sort(key=lambda t: -min(t[0], 4 - t[0]) - min(t[1], 8 - t[1]))
+LINE = sorted(range(1, 24), key=lambda i: -min(i, 24 - i))
+
 
 def device(dx, dy, dz):
     return tuple(
         lax.rem(lax.axis_index(axis) + (step + count), count)
         for axis, step, count in zip(AXES, (dx, dy, dz), GROUPS)
     )
-
-
-def partner():
-    place = lax.axis_index("gx")
-    return (place + 1 - 2 * lax.rem(place, 2), lax.axis_index("gy"), lax.axis_index("gz"))
 
 
 def zp(v):
@@ -502,18 +501,19 @@
             fixed_part = d * d if fixed_part is None else fixed_part + d * d
         b = b + (1.0 - free[p][0:8, 0:128]) * fixed_part
         denominator = b if denominator is None else denominator + b
-    numerator = numerator + pltpu.roll(numerator, 4, 0)
-    denominator = denominator + pltpu.roll(denominator, 4, 0)
-    sums = jnp.where(top_half, numerator, denominator)
+    numerator = jnp.sum(numerator, axis=0, keepdims=True)
+    denominator = jnp.sum(denominator, axis=0, keepdims=True)
+    sums = jnp.concatenate([numerator, denominator], 0)
 
     landed = [0]
+    pair = pl.ds(0, 2)
 
     def spread_sums(stage, value, targets):
-        ar_send[stage] = value
+        ar_send[stage, 0:2] = value
         base = landed[0]
         landed[0] += len(targets)
         group = [
-            send(ar_send.at[stage], ar_land.at[base + n], target)
+            send(ar_send.at[stage, pair], ar_land.at[base + n, pair], target)
             for n, target in enumerate(targets)
         ]
 
@@ -521,13 +521,12 @@
             arrive(group)
             total = value
             for n in range(len(targets)):
-                total = total + ar_land[base + n]
+                total = total + ar_land[base + n, 0:2]
             return total
 
         return gather
 
-    sums = spread_sums(0, sums, [partner()])()
-    gather = spread_sums(1, sums, [device(0, 0, k) for k in (4, 3, 5, 2, 6, 1, 7)])
+    gather = spread_sums(0, sums, [device(0, j, k) for j, k in FLAT])
     arrive(group2)
 
     edges2 = [jnp.concatenate([lz2[0, n], lc2[0, n]], 0) for n in range(2)]
@@ -570,9 +569,8 @@
         for c in range(3):
             image_out[c, p] = image[p][c][0:8, 0:128]
     sums = gather()
-    sums = spread_sums(2, sums, [device(0, j, 0) for j in (2, 1, 3)])()
     pl.semaphore_wait(relay_sem.at[3], 2)
-    gather = spread_sums(3, sums, [device(2 * i, 0, 0) for i in (6, 5, 7, 4, 8, 3, 9, 2, 10, 1, 11)])
+    gather = spread_sums(1, sums, [device(i, 0, 0) for i in LINE])
     arrive(near)
     arrive(far)
     edges3 = [edges_of(land3, slot, 0) for slot in range(3)]
@@ -588,9 +586,8 @@
             grads_out[f, p] = v[0:8, 0:128]
     settle()
     sums = gather()
-    numerator = jnp.sum(jnp.where(top_half, sums, 0.0), axis=(0, 1), keepdims=True)
-    denominator = jnp.sum(jnp.where(top_half, 0.0, sums), axis=(0, 1), keepdims=True)
-    step_out[...] = jnp.broadcast_to(numerator / denominator, (8, 128))
+    sums = jnp.sum(sums, axis=1, keepdims=True)
+    step_out[...] = jnp.broadcast_to(sums[0:1] / sums[1:2], (8, 128))
     settle()
 
 
@@ -606,7 +603,7 @@
             scratch(3, 4, packs, 8, 128),
         ]
 
-    n_copies = 3 * 26 + 7 + 22
+    n_copies = 3 * 26 + 7 + 54
     direction, image, grads, step = pl.pallas_call(
         kernel,
         out_shape=(
@@ -637,8 +634,8 @@
             scratch(8, 8, 128),
             scratch(1, 8, 128),
             *landing(8, 1),
-            scratch(4, 8, 128),
-            scratch(22, 8, 128),
+            scratch(2, 8, 128),
+            scratch(54, 8, 128),
             pltpu.SemaphoreType.DMA((n_copies,)),
             pltpu.SemaphoreType.DMA((n_copies,)),
             pltpu.SemaphoreType.REGULAR((4,)),

time: 49.6 us -> 48.2 us (0.972)
  the two profiles are of different devices: /device:TPU:2 before, /device:TPU:1 now
where the time goes in v5:
time: 48.2 us; the launch traced here: 47.9 us
  Pallas kernels  45.9 us (95%)
  other arithmetic  1.27 us (3%)
  between operations  0.68 us (1%)
    pallas_call x1, Pallas kernels, body(): pl.pallas_call(kernel, out_shape=(pltpu.VMEM((3, 4, 8, 128), jnp.float32)...  45.9 us

profile of v5, /device:TPU:1, one launch (start us, length us, event | category | flops | bytes accessed | tf_op | source)
XLA Modules:
  0.0 47.9 jit_solution(11085793181531419081)
XLA Ops:
  0.6 0.0 copy-start
  0.6 0.0 copy-start.1
  0.7 45.9 %shard_map.85 = (f32[3,4,8,128]{3,2,1,0:T(8,128)S(1)}, f32[3,4,8,128]{3,2,1,0:T(8,128)S(1)}, f32[2,4,8,128]{3,2,1,0:T(8,128)S(1)}, f32[8,128]{1,0:T(8,128)S(1)}) custom-call(f32[4,8,128]{2,1,0:T(8,128)} %design_hbm.1, s32[4,8,128]{2,1,0:T(8,128)} %passive_hbm.1, s32[4,8,128]{2,1,0:T(8,128)} %fixed_hbm.1, f32[3,4,8,128]{3,2,1,0:T(8,128)} %state_hbm.1, ...), custom_call_target="tpu_custom_call" | custom-call | tf_op jit(solution)/shard_map/pallas_call | solution.py:607
  46.6 0.0 copy-done
  46.6 0.0 copy-done.1
  46.6 0.0 copy-start.2
  46.6 0.7 %multiply_subtract_fusion = (f32[3,4,8,128]{3,2,1,0:T(8,128)}, f32[3,4,8,128]{3,2,1,0:T(8,128)}) fusion(f32[3,4,8,128]{3,2,1,0:T(8,128)S(1)} %copy-done, f32[3,4,8,128]{3,2,1,0:T(8,128)S(1)} %get-tuple-element.9, f32[8,128]{1,0:T(8,128)S(1)} %get-tuple-element.7, f32[3,4,8,128]{3,2,1,0:T(8,128)S(1)} %copy-done.1, f32[3,4,8,128]{3,2,1,0:T(8,128)S(1)} %get-tuple-element.8), kind=kLoop, calls=%fused_computation | loop fusion | flops 49152 | bytes 299008 | tf_op jit(solution)/shard_map/sub | solution.py:649
  47.2 0.0 copy-done.2
  47.3 0.6 %fusion.1 = f32[4,8,128]{2,1,0:T(8,128)} fusion(f32[2,4,8,128]{3,2,1,0:T(8,128)S(1)} %get-tuple-element.10, s32[4,8,128]{2,1,0:T(8,128)S(1)} %copy-done.2, f32[8,128]{1,0:T(8,128)S(1)} %get-tuple-element.7), kind=kLoop, calls=%fused_computation.4 | loop fusion | flops 16384 | bytes 69632 | tf_op jit(solution)/shard_map/jit(_where)/select_n | solution.py:650
Async XLA Ops:
  0.6 45.9 %copy-start = (f32[3,4,8,128]{3,2,1,0:T(8,128)S(1)}, f32[3,4,8,128]{3,2,1,0:T(8,128)}, u32[]{:S(2)}) copy-start(f32[3,4,8,128]{3,2,1,0:T(8,128)} %resid_hbm.1) | copy-start | bytes 147460
  0.6 45.9 %copy-start.1 = (f32[3,4,8,128]{3,2,1,0:T(8,128)S(1)}, f32[3,4,8,128]{3,2,1,0:T(8,128)}, u32[]{:S(2)}) copy-start(f32[3,4,8,128]{3,2,1,0:T(8,128)} %adjoint_hbm.1) | copy-start | bytes 147460
  46.6 0.7 %copy-start.2 = (s32[4,8,128]{2,1,0:T(8,128)S(1)}, s32[4,8,128]{2,1,0:T(8,128)}, u32[]{:S(2)}) copy-start(s32[4,8,128]{2,1,0:T(8,128)} %passive_hbm.1) | copy-start | bytes 49156

commit v6 on v5

--- a/solution.py
+++ b/solution.py
@@ -314,7 +314,8 @@
                     copy = send(edges.at[span], land_z.at[slot, (k + 1) // 2, span], target)
                 else:
                     corner = j + 1 + (k + 1) // 2
-                    copy = send(edges.at[span], land_c.at[slot, corner, span], target)
+                    half = pl.ds(2 * (j + 1), 4)
+                    copy = send(edges.at[span, half], land_c.at[slot, corner, span, half], target)
             (near if i == 0 else far).append(copy)
         return near, far
 
@@ -501,15 +502,18 @@
             fixed_part = d * d if fixed_part is None else fixed_part + d * d
         b = b + (1.0 - free[p][0:8, 0:128]) * fixed_part
         denominator = b if denominator is None else denominator + b
-    numerator = jnp.sum(numerator, axis=0, keepdims=True)
-    denominator = jnp.sum(denominator, axis=0, keepdims=True)
-    sums = jnp.concatenate([numerator, denominator], 0)
+    sums = jnp.where(
+        iota((8, 128), 1) < 64,
+        numerator + pltpu.roll(numerator, 64, 1),
+        denominator + pltpu.roll(denominator, 64, 1),
+    )
+    sums = jnp.sum(sums, axis=0, keepdims=True)
 
     landed = [0]
-    pair = pl.ds(0, 2)
+    pair = pl.ds(0, 1)
 
     def spread_sums(stage, value, targets):
-        ar_send[stage, 0:2] = value
+        ar_send[stage, 0:1] = value
         base = landed[0]
         landed[0] += len(targets)
         group = [
@@ -521,7 +525,7 @@
             arrive(group)
             total = value
             for n in range(len(targets)):
-                total = total + ar_land[base + n, 0:2]
+                total = total + ar_land[base + n, 0:1]
             return total
 
         return gather
@@ -586,8 +590,10 @@
             grads_out[f, p] = v[0:8, 0:128]
     settle()
     sums = gather()
-    sums = jnp.sum(sums, axis=1, keepdims=True)
-    step_out[...] = jnp.broadcast_to(sums[0:1] / sums[1:2], (8, 128))
+    first_half = iota((1, 128), 1) < 64
+    numerator = jnp.sum(jnp.where(first_half, sums, 0.0), axis=1, keepdims=True)
+    denominator = jnp.sum(jnp.where(first_half, 0.0, sums), axis=1, keepdims=True)
+    step_out[...] = jnp.broadcast_to(numerator / denominator, (8, 128))
     settle()
 
 

time: 48.2 us -> 47.8 us (level)
  no operation moved by 1% of the time
where the time goes in v6:
time: 47.8 us; the launch traced here: 47.5 us
  Pallas kernels  45.5 us (95%)
  other arithmetic  1.27 us (3%)
  between operations  0.68 us (1%)
    pallas_call x1, Pallas kernels, body(): pl.pallas_call(kernel, out_shape=(pltpu.VMEM((3, 4, 8, 128), jnp.float32)...  45.5 us

profile of v6, /device:TPU:1, one launch (start us, length us, event | category | flops | bytes accessed | tf_op | source)
XLA Modules:
  0.0 47.5 jit_solution(3424013732393319141)
XLA Ops:
  0.6 0.0 copy-start
  0.6 0.0 copy-start.1
  0.7 45.5 %shard_map.85 = (f32[3,4,8,128]{3,2,1,0:T(8,128)S(1)}, f32[3,4,8,128]{3,2,1,0:T(8,128)S(1)}, f32[2,4,8,128]{3,2,1,0:T(8,128)S(1)}, f32[8,128]{1,0:T(8,128)S(1)}) custom-call(f32[4,8,128]{2,1,0:T(8,128)} %design_hbm.1, s32[4,8,128]{2,1,0:T(8,128)} %passive_hbm.1, s32[4,8,128]{2,1,0:T(8,128)} %fixed_hbm.1, f32[3,4,8,128]{3,2,1,0:T(8,128)} %state_hbm.1, ...), custom_call_target="tpu_custom_call" | custom-call | tf_op jit(solution)/shard_map/pallas_call | solution.py:613
  46.1 0.0 copy-done
  46.1 0.0 copy-done.1
  46.1 0.0 copy-start.2
  46.1 0.7 %multiply_subtract_fusion = (f32[3,4,8,128]{3,2,1,0:T(8,128)}, f32[3,4,8,128]{3,2,1,0:T(8,128)}) fusion(f32[3,4,8,128]{3,2,1,0:T(8,128)S(1)} %copy-done, f32[3,4,8,128]{3,2,1,0:T(8,128)S(1)} %get-tuple-element.9, f32[8,128]{1,0:T(8,128)S(1)} %get-tuple-element.7, f32[3,4,8,128]{3,2,1,0:T(8,128)S(1)} %copy-done.1, f32[3,4,8,128]{3,2,1,0:T(8,128)S(1)} %get-tuple-element.8), kind=kLoop, calls=%fused_computation | loop fusion | flops 49152 | bytes 299008 | tf_op jit(solution)/shard_map/sub | solution.py:655
  46.8 0.0 copy-done.2
  46.9 0.6 %fusion.1 = f32[4,8,128]{2,1,0:T(8,128)} fusion(f32[2,4,8,128]{3,2,1,0:T(8,128)S(1)} %get-tuple-element.10, s32[4,8,128]{2,1,0:T(8,128)S(1)} %copy-done.2, f32[8,128]{1,0:T(8,128)S(1)} %get-tuple-element.7), kind=kLoop, calls=%fused_computation.4 | loop fusion | flops 16384 | bytes 69632 | tf_op jit(solution)/shard_map/jit(_where)/select_n | solution.py:656
Async XLA Ops:
  0.6 45.5 %copy-start = (f32[3,4,8,128]{3,2,1,0:T(8,128)S(1)}, f32[3,4,8,128]{3,2,1,0:T(8,128)}, u32[]{:S(2)}) copy-start(f32[3,4,8,128]{3,2,1,0:T(8,128)} %resid_hbm.1) | copy-start | bytes 147460
  0.6 45.5 %copy-start.1 = (f32[3,4,8,128]{3,2,1,0:T(8,128)S(1)}, f32[3,4,8,128]{3,2,1,0:T(8,128)}, u32[]{:S(2)}) copy-start(f32[3,4,8,128]{3,2,1,0:T(8,128)} %adjoint_hbm.1) | copy-start | bytes 147460
  46.1 0.7 %copy-start.2 = (s32[4,8,128]{2,1,0:T(8,128)S(1)}, s32[4,8,128]{2,1,0:T(8,128)}, u32[]{:S(2)}) copy-start(s32[4,8,128]{2,1,0:T(8,128)} %passive_hbm.1) | copy-start | bytes 49156
